TPU v7x, 32 devices: a whole 2x2x4 slice. The times are simulated.
32 devices in a mesh: grp: 2 (over y), row: 4 (over x, core), col: 4 (over z).
Axes of the slice: x: 2, y: 2, z: 4, core: 2. Of those that a mesh axis runs over, the one named last changes fastest.
Arguments:
- level_one: bfloat16 [128, 256, 192], P(('grp', 'row'), 'col'), parts along dimension 0, may hold values from -6 to 6
- level_two: bfloat16 [64, 128, 384], P(('grp', 'row'), 'col'), parts along dimension 0, may hold values from -6 to 6
- level_three: bfloat16 [32, 64, 768], P(('grp', 'row'), None, 'col'), parts along dimension 0, may hold values from -6 to 6
- level_four: bfloat16 [16, 32, 1536], P(('grp', 'row'), None, 'col'), parts along dimension 0, may hold values from -10.5 to 10.5
- bin_weight: bfloat16 [4, 1536, 256], P(None, 'col'), may hold values from -0.21875 to 0.21875
- neck_feature: bfloat16 [3, 3, 1536, 256], P(None, None, 'col'), may hold values from -0.0546875 to 0.0546875
- neck_pooled: bfloat16 [3, 3, 1024, 256], P(None, None, 'col'), may hold values from -0.0546875 to 0.0546875
- lateral_one: bfloat16 [192, 256], replicated, may hold values from -0.625 to 0.625
- lateral_two: bfloat16 [384, 256], replicated, may hold values from -0.4375 to 0.4375
- lateral_three: bfloat16 [768, 256], replicated, may hold values from -0.3125 to 0.3125
- smooth_weight: bfloat16 [3, 3, 3, 256, 256], replicated, may hold values from -0.1875 to 0.1875
- join_weight: bfloat16 [3, 3, 1024, 256], replicated, may hold values from -0.09375 to 0.09375
- biases: float32 [12, 256], replicated, may hold values from -2 to 2
Outputs:
- joined: bfloat16 [128, 256, 256], P(('grp', 'row'), 'col'), parts along dimension 0
There are 2 independent parts, one for each index of `grp`. A program takes and returns all parts, laid end to end along the dimension named above; an argument that names none is the same for every part. Nothing has to cross between parts.
All inputs are finite; a program needn't handle non-finite values.
Results may differ from a plain program's by a relative error of at most 0.015.
Values may be sent and summed in bfloat16 or wider, within the bound.
A program may use at most 64 MiB of HBM per device.

v0:
```python
import jax
import jax.numpy as jnp
from jax import lax
from jax.sharding import PartitionSpec as P

highest = lax.Precision.HIGHEST
bin_sides = (1, 2, 3, 6)


def with_halo(block, sides, width):
    for axis, dim in sides:
        count = lax.axis_size(axis)
        forward = [(i, i + 1) for i in range(count - 1)]
        backward = [(target, source) for source, target in forward]
        low = lax.ppermute(
            lax.slice_in_dim(block, block.shape[dim] - width, None, axis=dim), axis, forward
        )
        high = lax.ppermute(lax.slice_in_dim(block, 0, width, axis=dim), axis, backward)
        block = jnp.concatenate([low, block, high], axis=dim)
    return block


def pool_matrix(bin_side, extent, first, length):
    cell_index = jnp.arange(bin_side, dtype=jnp.int32)[:, None]
    position = first + jnp.arange(length, dtype=jnp.int32)[None, :]
    cell_first = cell_index * extent // bin_side
    cell_end = ((cell_index + 1) * extent + bin_side - 1) // bin_side
    inside = (position >= cell_first) & (position < cell_end)
    return inside.astype(jnp.float32) / (cell_end - cell_first).astype(jnp.float32)


def stretch_rows(position, bin_side, extent):
    source = jnp.clip((position + 0.5) * bin_side / extent - 0.5, 0.0, bin_side - 1.0)
    targets = jnp.arange(bin_side, dtype=jnp.float32)[None, :]
    return jnp.maximum(0.0, 1.0 - jnp.abs(source[:, None] - targets))


def tile_rim(feature):
    return with_halo(feature, (("row", 0), ("col", 1)), 1)


def clamp_edges(padded):
    row_here = lax.axis_index("row")
    row_last = lax.axis_size("row") - 1
    top_edge = jnp.where(row_here == 0, padded[1:2], padded[0:1])
    bottom_edge = jnp.where(row_here == row_last, padded[-2:-1], padded[-1:])
    padded = jnp.concatenate([top_edge, padded[1:-1], bottom_edge], axis=0)
    col_here = lax.axis_index("col")
    col_last = lax.axis_size("col") - 1
    left_edge = jnp.where(col_here == 0, padded[:, 1:2], padded[:, 0:1])
    right_edge = jnp.where(col_here == col_last, padded[:, -2:-1], padded[:, -1:])
    return jnp.concatenate([left_edge, padded[:, 1:-1], right_edge], axis=1)


def local_stretch(length, factor, border):
    output = jnp.arange(length * factor + 2 * border, dtype=jnp.float32) - border
    position = (output + 0.5) / factor + 0.5
    targets = jnp.arange(length + 2, dtype=jnp.float32)[None, :]
    return jnp.maximum(0.0, 1.0 - jnp.abs(position[:, None] - targets))


def upscale_rimmed(padded, factor, border):
    height = padded.shape[0] - 2
    breadth = padded.shape[1] - 2
    clamped = clamp_edges(padded).astype(jnp.float32)
    result = jnp.einsum(
        "oh,hwc->owc", local_stretch(height, factor, border), clamped, precision=highest
    )
    return jnp.einsum(
        "pw,owc->opc", local_stretch(breadth, factor, border), result, precision=highest
    )


def taps_sum(padded, weight):
    height = padded.shape[0] - 2
    breadth = padded.shape[1] - 2
    channels = padded.shape[2]
    summed = jnp.zeros((height * breadth, weight.shape[-1]), jnp.float32)
    for row_tap in range(3):
        for col_tap in range(3):
            window = padded[row_tap : row_tap + height, col_tap : col_tap + breadth].reshape(
                height * breadth, channels
            )
            summed = summed + jnp.dot(
                window, weight[row_tap, col_tap], preferred_element_type=jnp.float32
            )
    return summed.reshape(height, breadth, -1)


def project(feature, weight):
    height, breadth, channels = feature.shape
    result = jnp.dot(
        feature.reshape(height * breadth, channels), weight, preferred_element_type=jnp.float32
    )
    return result.reshape(height, breadth, -1)


def local(
    level_one,
    level_two,
    level_three,
    level_four,
    bin_weight,
    neck_feature,
    neck_pooled,
    lateral_one,
    lateral_two,
    lateral_three,
    smooth_weight,
    join_weight,
    biases,
):
    row_here = lax.axis_index("row")
    col_here = lax.axis_index("col")
    strip_rows, grid_cols, part_four = level_four.shape
    grid_rows = strip_rows * lax.axis_size("row")
    first_row = row_here * strip_rows
    out_channels = bin_weight.shape[2]
    coarse = level_four.astype(jnp.float32)
    pooled_parts = []
    cell_offsets = [0]
    for bin_side in bin_sides:
        pool_down = pool_matrix(bin_side, grid_rows, first_row, strip_rows)
        pool_across = pool_matrix(bin_side, grid_cols, 0, grid_cols)
        pooled = jnp.einsum("ih,hwc->iwc", pool_down, coarse, precision=highest)
        pooled = jnp.einsum("jw,iwc->ijc", pool_across, pooled, precision=highest)
        pooled_parts.append(pooled.reshape(bin_side * bin_side, part_four))
        cell_offsets.append(cell_offsets[-1] + bin_side * bin_side)
    bin_local = bin_weight.astype(jnp.float32)

    def bin_terms(pooled_list):
        return jnp.concatenate(
            [
                jnp.dot(pooled_list[number], bin_local[number], precision=highest)
                for number in range(len(bin_sides))
            ],
            axis=0,
        )

    pooled_whole = lax.psum(
        jnp.concatenate(pooled_parts, axis=0).astype(jnp.bfloat16), "row"
    ).astype(jnp.float32)
    pooled_split = [
        pooled_whole[cell_offsets[number] : cell_offsets[number + 1]]
        for number in range(len(bin_sides))
    ]
    bin_total = lax.psum(bin_terms(pooled_split).astype(jnp.bfloat16), "col").astype(jnp.float32)
    down_place = (first_row - 1 + jnp.arange(strip_rows + 2, dtype=jnp.int32)).astype(jnp.float32)
    inside_grid = ((down_place >= 0.0) & (down_place < grid_rows)).astype(jnp.float32)
    across_place = jnp.arange(grid_cols, dtype=jnp.float32)
    bin_maps = []
    for number, bin_side in enumerate(bin_sides):
        cell_values = bin_total[cell_offsets[number] : cell_offsets[number + 1]].reshape(
            bin_side, bin_side, out_channels
        )
        binned = jax.nn.relu(cell_values + biases[number])
        stretch_down = stretch_rows(down_place, bin_side, grid_rows) * inside_grid[:, None]
        stretch_across = stretch_rows(across_place, bin_side, grid_cols)
        spread = jnp.einsum("hi,ijd->hjd", stretch_down, binned, precision=highest)
        spread = jnp.einsum("wj,hjd->hwd", stretch_across, spread, precision=highest)
        bin_maps.append(spread)
    ppm_maps = jnp.concatenate(bin_maps, axis=2).astype(jnp.bfloat16)
    share_ppm = neck_pooled.shape[2]
    ppm_maps = lax.dynamic_slice_in_dim(ppm_maps, col_here * share_ppm, share_ppm, 2)
    feature_rim = with_halo(level_four, (("row", 0),), 1)
    stacked = jnp.concatenate([feature_rim, ppm_maps], axis=2)
    stacked = jnp.pad(stacked, ((0, 0), (1, 1), (0, 0)))
    neck_weight = jnp.concatenate([neck_feature, neck_pooled], axis=2)
    neck_term = taps_sum(stacked, neck_weight)
    share_three = level_three.shape[2]
    weight_three = lax.dynamic_slice_in_dim(lateral_three, col_here * share_three, share_three, 0)
    three_term = project(level_three, weight_three)
    three_sum, top_sum = (
        lax.psum_scatter(
            three_term.astype(jnp.bfloat16), "col", scatter_dimension=1, tiled=True
        ).astype(jnp.float32),
        lax.psum_scatter(
            neck_term.astype(jnp.bfloat16), "col", scatter_dimension=1, tiled=True
        ).astype(jnp.float32),
    )
    pyramid_four = jax.nn.relu(top_sum + biases[4]).astype(jnp.bfloat16)
    rimmed_four = tile_rim(pyramid_four)
    pyramid_three = (jax.nn.relu(three_sum + biases[7]) + upscale_rimmed(rimmed_four, 2, 0)).astype(
        jnp.bfloat16
    )
    rimmed_three = tile_rim(pyramid_three)
    pyramid_two = (
        jax.nn.relu(project(level_two, lateral_two) + biases[6])
        + upscale_rimmed(rimmed_three, 2, 0)
    ).astype(jnp.bfloat16)
    rimmed_two = tile_rim(pyramid_two)
    pyramid_one = (
        jax.nn.relu(project(level_one, lateral_one) + biases[5]) + upscale_rimmed(rimmed_two, 2, 0)
    ).astype(jnp.bfloat16)
    smooth_one = jax.nn.relu(taps_sum(tile_rim(pyramid_one), smooth_weight[0]) + biases[8]).astype(
        jnp.bfloat16
    )
    smooth_two = jax.nn.relu(taps_sum(rimmed_two, smooth_weight[1]) + biases[9]).astype(
        jnp.bfloat16
    )
    smooth_three = jax.nn.relu(taps_sum(rimmed_three, smooth_weight[2]) + biases[10]).astype(
        jnp.bfloat16
    )
    stacked_top = jnp.concatenate(
        [
            smooth_one,
            upscale_rimmed(tile_rim(smooth_two), 2, 0).astype(jnp.bfloat16),
            upscale_rimmed(tile_rim(smooth_three), 4, 0).astype(jnp.bfloat16),
            upscale_rimmed(rimmed_four, 8, 0).astype(jnp.bfloat16),
        ],
        axis=2,
    )
    framed = tile_rim(stacked_top)
    return jax.nn.relu(taps_sum(framed, join_weight) + biases[11]).astype(jnp.bfloat16)


def solution(mesh):
    placed = (
        P(("grp", "row"), "col", None),
        P(("grp", "row"), "col", None),
        P(("grp", "row"), None, "col"),
        P(("grp", "row"), None, "col"),
        P(None, "col", None),
        P(None, None, "col", None),
        P(None, None, "col", None),
        P(),
        P(),
        P(),
        P(),
        P(),
        P(),
    )
    return jax.shard_map(
        local, mesh=mesh, in_specs=placed, out_specs=P(("grp", "row"), "col", None), check_vma=False
    )
```

profile of v0, /device:TPU:0, one launch (start us, length us, event | category | flops | bytes accessed | tf_op | source)
XLA Modules:
  0.0 223.5 jit_solution(17948178878431407120)
XLA Ops:
  6.5 1.5 fusion.376
  8.0 2.9 %collective-permute-start = (bf16[1,32,384]{2,1,0:T(8,128)(2,1)}, bf16[1,32,384]{2,1,0:T(8,128)(2,1)}, u32[]{:S(2)}, u32[]{:S(2)}) collective-permute-start(bf16[1,32,384]{2,1,0:T(8,128)(2,1)} %get-tuple-element.83), channel_id=1, source_target_pairs={{0,4},{4,8},{8,12},{1,5},{5,9},{9,13},{2,6},{6,10},{10,14},{3,7},{... | collective-permute-start | bytes 73736 | tf_op jit(solution)/shard_map/ppermute | solution.py:15
  19.8 13.7 %psum.14 = bf16[50,384]{1,0:T(8,128)(2,1)S(1)} all-reduce(bf16[50,384]{1,0:T(8,128)(2,1)S(1)} %pad_maximum_fusion.36), channel_id=1, replica_groups=mesh['grp'=2,'row'=4,'col'=4] {'row'}, use_global_device_ids=true, to_apply=%region_1.2 | all-reduce | flops 19200 | bytes 76800 | tf_op jit(solution)/shard_map/psum | solution.py:140
  34.1 19.2 %psum.15 = bf16[50,256]{1,0:T(8,128)(2,1)S(1)} all-reduce(bf16[50,256]{1,0:T(8,128)(2,1)S(1)} %pad_maximum_fusion.42), channel_id=1, replica_groups=mesh['grp'=2,'row'=4,'col'=4] {'col'}, use_global_device_ids=true, to_apply=%region_2.3 | all-reduce | flops 12800 | bytes 51200 | tf_op jit(solution)/shard_map/psum | solution.py:147
  54.7 1.6 constant_dynamic-update-slice_fusion.1
  70.9 1.8 convolution_convert_fusion.3
  72.9 3.3 %slice_bitcast_fusion.2 = (bf16[3,3,256,256]{3,2,1,0:T(8,128)(2,1)}, bf16[3,3,256,256]{3,2,1,0:T(8,128)(2,1)S(1)}, bf16[3,3,256,256]{3,2,1,0:T(8,128)(2,1)S(1)}) fusion(bf16[3,3,3,256,256]{4,3,2,1,0:T(8,128)(2,1)} %param.23), kind=kLoop, calls=%fused_computation.40 | loop fusion | bytes 7077888 | tf_op jit(solution)/shard_map/squeeze | solution.py:195
  77.5 10.4 %reduce-scatter.7.cloned.1.call-done = bf16[8,512]{1,0:T(8,128)(2,1)} async-done(((bf16[32,512]{1,0:T(8,128)(2,1)}), bf16[8,512]{1,0:T(8,128)(2,1)}) %reduce-scatter.7.cloned.1.call-update) | async-done | bytes 8208
  91.2 3.4 %collective-permute-done.3 = bf16[1,8,256]{2,1,0:T(8,128)(2,1)S(1)} collective-permute-done((bf16[1,8,256]{2,1,0:T(8,128)(2,1)S(1)}, bf16[1,8,256]{2,1,0:T(8,128)(2,1)S(1)}, u32[]{:S(2)}, u32[]{:S(2)}) %collective-permute-start.3) | collective-permute-done | bytes 4128 | tf_op jit(solution)/shard_map/ppermute | solution.py:18
  97.3 4.2 %collective-permute-done.5 = bf16[4,1,256]{2,1,0:T(2,128)(2,1)S(1)} collective-permute-done((bf16[4,1,256]{2,1,0:T(2,128)(2,1)S(1)}, bf16[4,1,256]{2,1,0:T(2,128)(2,1)S(1)}, u32[]{:S(2)}, u32[]{:S(2)}) %collective-permute-start.5) | collective-permute-done | bytes 2080 | tf_op jit(solution)/shard_map/ppermute | solution.py:18
  102.1 5.4 %reduce-scatter.5.cloned.1.call-done = bf16[4,16,256]{2,1,0:T(8,128)(2,1)} async-done(((bf16[4,64,256]{2,1,0:T(8,128)(2,1)}), bf16[4,16,256]{2,1,0:T(8,128)(2,1)}) %reduce-scatter.5.cloned.1.call-update) | async-done | bytes 32784 | tf_op jit(solution)/shard_map/reduce_scatter | solution.py:174
  112.3 2.4 %collective-permute-done.7 = bf16[1,16,256]{2,1,0:T(8,128)(2,1)S(1)} collective-permute-done((bf16[1,16,256]{2,1,0:T(8,128)(2,1)S(1)}, bf16[1,16,256]{2,1,0:T(8,128)(2,1)S(1)}, u32[]{:S(2)}, u32[]{:S(2)}) %collective-permute-start.7) | collective-permute-done | bytes 8224 | tf_op jit(solution)/shard_map/ppermute | solution.py:18
  117.4 4.1 %collective-permute-done.9 = bf16[6,1,256]{2,1,0:T(2,128)(2,1)S(1)} collective-permute-done((bf16[6,1,256]{2,1,0:T(2,128)(2,1)S(1)}, bf16[6,1,256]{2,1,0:T(2,128)(2,1)S(1)}, u32[]{:S(2)}, u32[]{:S(2)}) %collective-permute-start.9) | collective-permute-done | bytes 3104 | tf_op jit(solution)/shard_map/ppermute | solution.py:18
  123.1 3.2 %collective-permute-start.22 = (bf16[1,16,256]{2,1,0:T(8,128)(2,1)S(1)}, bf16[1,16,256]{2,1,0:T(8,128)(2,1)S(1)}, u32[]{:S(2)}, u32[]{:S(2)}) collective-permute-start(bf16[1,16,256]{2,1,0:T(8,128)(2,1)S(1)} %get-tuple-element.85), channel_id=1, source_target_pairs={{0,4},{4,8},{8,12},{1,5},{5,9},{9,13},{2,6},{6,10},{10,14},{3,7},{... | collective-permute-start | bytes 24584 | tf_op jit(solution)/shard_map/ppermute | solution.py:15
  130.0 3.7 %collective-permute-start.24 = (bf16[6,1,256]{2,1,0:T(2,128)(2,1)S(1)}, bf16[6,1,256]{2,1,0:T(2,128)(2,1)S(1)}, u32[]{:S(2)}, u32[]{:S(2)}) collective-permute-start(bf16[6,1,256]{2,1,0:T(2,128)(2,1)S(1)} %get-tuple-element.77), channel_id=1, source_target_pairs={{0,1},{1,2},{2,3},{4,5},{5,6},{6,7},{8,9},{9,10},{10,11},{12,13},{... | collective-permute-start | bytes 9224 | tf_op jit(solution)/shard_map/ppermute | solution.py:15
  135.0 4.0 %collective-permute-start.10 = (bf16[1,32,256]{2,1,0:T(8,128)(2,1)S(1)}, bf16[1,32,256]{2,1,0:T(8,128)(2,1)S(1)}, u32[]{:S(2)}, u32[]{:S(2)}) collective-permute-start(bf16[1,32,256]{2,1,0:T(8,128)(2,1)S(1)} %get-tuple-element.65), channel_id=1, source_target_pairs={{0,4},{4,8},{8,12},{1,5},{5,9},{9,13},{2,6},{6,10},{10,14},{3,7},{... | collective-permute-start | bytes 49160 | tf_op jit(solution)/shard_map/ppermute | solution.py:15
  142.2 4.4 %collective-permute-start.12 = (bf16[10,1,256]{2,1,0:T(2,128)(2,1)S(1)}, bf16[10,1,256]{2,1,0:T(2,128)(2,1)S(1)}, u32[]{:S(2)}, u32[]{:S(2)}) collective-permute-start(bf16[10,1,256]{2,1,0:T(2,128)(2,1)S(1)} %get-tuple-element.50), channel_id=1, source_target_pairs={{0,1},{1,2},{2,3},{4,5},{5,6},{6,7},{8,9},{9,10},{10,11},{12,13},{... | collective-permute-start | bytes 15368 | tf_op jit(solution)/shard_map/ppermute | solution.py:15
  146.6 1.5 collective-permute-start.13
  148.3 3.9 %collective-permute-done.13 = bf16[10,1,256]{2,1,0:T(2,128)(2,1)S(1)} collective-permute-done((bf16[10,1,256]{2,1,0:T(2,128)(2,1)S(1)}, bf16[10,1,256]{2,1,0:T(2,128)(2,1)S(1)}, u32[]{:S(2)}, u32[]{:S(2)}) %collective-permute-start.13) | collective-permute-done | bytes 5152 | tf_op jit(solution)/shard_map/ppermute | solution.py:18
  154.8 3.0 %collective-permute-start.18 = (bf16[1,32,256]{2,1,0:T(8,128)(2,1)S(1)}, bf16[1,32,256]{2,1,0:T(8,128)(2,1)S(1)}, u32[]{:S(2)}, u32[]{:S(2)}) collective-permute-start(bf16[1,32,256]{2,1,0:T(8,128)(2,1)S(1)} %get-tuple-element.61), channel_id=1, source_target_pairs={{0,4},{4,8},{8,12},{1,5},{5,9},{9,13},{2,6},{6,10},{10,14},{3,7},{... | collective-permute-start | bytes 49160 | tf_op jit(solution)/shard_map/ppermute | solution.py:15
  160.4 1.6 collective-permute-done.19
  162.1 2.4 %collective-permute-start.20 = (bf16[10,1,256]{2,1,0:T(2,128)(2,1)S(1)}, bf16[10,1,256]{2,1,0:T(2,128)(2,1)S(1)}, u32[]{:S(2)}, u32[]{:S(2)}) collective-permute-start(bf16[10,1,256]{2,1,0:T(2,128)(2,1)S(1)} %get-tuple-element.46), channel_id=1, source_target_pairs={{0,1},{1,2},{2,3},{4,5},{5,6},{6,7},{8,9},{9,10},{10,11},{12,13},{... | collective-permute-start | bytes 15368 | tf_op jit(solution)/shard_map/ppermute | solution.py:15
  165.8 4.1 %collective-permute-start.14 = (bf16[1,64,256]{2,1,0:T(8,128)(2,1)S(1)}, bf16[1,64,256]{2,1,0:T(8,128)(2,1)S(1)}, u32[]{:S(2)}, u32[]{:S(2)}) collective-permute-start(bf16[1,64,256]{2,1,0:T(8,128)(2,1)S(1)} %get-tuple-element.34), channel_id=1, source_target_pairs={{0,4},{4,8},{8,12},{1,5},{5,9},{9,13},{2,6},{6,10},{10,14},{3,7},{... | collective-permute-start | bytes 98312 | tf_op jit(solution)/shard_map/ppermute | solution.py:15
  173.4 4.3 %collective-permute-start.16 = (bf16[18,1,256]{2,1,0:T(2,128)(2,1)S(1)}, bf16[18,1,256]{2,1,0:T(2,128)(2,1)S(1)}, u32[]{:S(2)}, u32[]{:S(2)}) collective-permute-start(bf16[18,1,256]{2,1,0:T(2,128)(2,1)S(1)} %get-tuple-element.30), channel_id=1, source_target_pairs={{0,1},{1,2},{2,3},{4,5},{5,6},{6,7},{8,9},{9,10},{10,11},{12,13},{... | collective-permute-start | bytes 27656 | tf_op jit(solution)/shard_map/ppermute | solution.py:15
  179.4 4.0 %collective-permute-done.17 = bf16[18,1,256]{2,1,0:T(2,128)(2,1)S(1)} collective-permute-done((bf16[18,1,256]{2,1,0:T(2,128)(2,1)S(1)}, bf16[18,1,256]{2,1,0:T(2,128)(2,1)S(1)}, u32[]{:S(2)}, u32[]{:S(2)}) %collective-permute-start.17) | collective-permute-done | bytes 9248 | tf_op jit(solution)/shard_map/ppermute | solution.py:18
  187.6 2.8 %collective-permute-start.26 = (bf16[1,64,1024]{2,1,0:T(8,128)(2,1)S(1)}, bf16[1,64,1024]{2,1,0:T(8,128)(2,1)S(1)}, u32[]{:S(2)}, u32[]{:S(2)}) collective-permute-start(bf16[1,64,1024]{2,1,0:T(8,128)(2,1)S(1)} %get-tuple-element.20), channel_id=1, source_target_pairs={{0,4},{4,8},{8,12},{1,5},{5,9},{9,13},{2,6},{6,10},{10,14},{3,7},{... | collective-permute-start | bytes 393224 | tf_op jit(solution)/shard_map/ppermute | solution.py:15
  192.4 2.8 %collective-permute-done.27 = bf16[1,64,1024]{2,1,0:T(8,128)(2,1)S(1)} collective-permute-done((bf16[1,64,1024]{2,1,0:T(8,128)(2,1)S(1)}, bf16[1,64,1024]{2,1,0:T(8,128)(2,1)S(1)}, u32[]{:S(2)}, u32[]{:S(2)}) %collective-permute-start.27) | collective-permute-done | bytes 131104 | tf_op jit(solution)/shard_map/ppermute | solution.py:18
  195.3 1.9 collective-permute-start.28
  197.2 1.5 collective-permute-start.29
  200.8 2.7 %collective-permute-done.29 = bf16[18,1,1024]{2,1,0:T(2,128)(2,1)S(1)} collective-permute-done((bf16[18,1,1024]{2,1,0:T(2,128)(2,1)S(1)}, bf16[18,1,1024]{2,1,0:T(2,128)(2,1)S(1)}, u32[]{:S(2)}, u32[]{:S(2)}) %collective-permute-start.29) | collective-permute-done | bytes 36896 | tf_op jit(solution)/shard_map/ppermute | solution.py:18
  203.5 5.5 %maximum_maximum_fusion = (bf16[18,65,1024]{2,1,0:T(8,128)(2,1)S(1)}, bf16[18,65,1024]{2,1,0:T(8,128)(2,1)S(1)}) fusion(bf16[1,64,1024]{2,1,0:T(8,128)(2,1)S(1)} %collective-permute-done.27, bf16[16,64,256]{2,1,0:T(8,128)(2,1)S(1)} %fusion.10, bf16[16,64,256]{2,1,0:T(8,128)(2,1)S(1)} %fusion.11, bf16[16,64,256]{2,1,0:T(8,128)(2,1)S(1)} %fusion.12, ...), kind=kLoop, calls=%fused_computation | loop fusion | flops 33546240 | bytes 7225344 | tf_op jit(solution)/shard_map/concatenate | solution.py:19
  211.3 1.5 fusion.364
  (288 shorter events, 75.9 us)
Async XLA Ops:
  6.5 81.3 %reduce-scatter.7.cloned.1.call-start = ((), (), s32[]{:S(2)}) async-start(), calls=%async_computation.3 | async-start | bytes 40960
  8.0 59.5 %collective-permute-start = (bf16[1,32,384]{2,1,0:T(8,128)(2,1)}, bf16[1,32,384]{2,1,0:T(8,128)(2,1)}, u32[]{:S(2)}, u32[]{:S(2)}) collective-permute-start(bf16[1,32,384]{2,1,0:T(8,128)(2,1)} %get-tuple-element.83), channel_id=1, source_target_pairs={{0,4},{4,8},{8,12},{1,5},{5,9},{9,13},{2,6},{6,10},{10,14},{3,7},{... | collective-permute-start | bytes 73736 | tf_op jit(solution)/shard_map/ppermute | solution.py:15
  11.0 56.6 %collective-permute-start.1 = (bf16[1,32,384]{2,1,0:T(8,128)(2,1)}, bf16[1,32,384]{2,1,0:T(8,128)(2,1)}, u32[]{:S(2)}, u32[]{:S(2)}) collective-permute-start(bf16[1,32,384]{2,1,0:T(8,128)(2,1)} %get-tuple-element.84), channel_id=1, source_target_pairs={{4,0},{8,4},{12,8},{5,1},{9,5},{13,9},{6,2},{10,6},{14,10},{7,3},{... | collective-permute-start | bytes 73736 | tf_op jit(solution)/shard_map/ppermute | solution.py:18
  70.9 36.7 %reduce-scatter.5.cloned.1.call-start = ((), (), s32[]{:S(2)}) async-start(), calls=%async_computation.2 | async-start | bytes 163840 | tf_op jit(solution)/shard_map/reduce_scatter | solution.py:174
  88.6 2.6 %collective-permute-start.2 = (bf16[1,8,256]{2,1,0:T(8,128)(2,1)S(1)}, bf16[1,8,256]{2,1,0:T(8,128)(2,1)S(1)}, u32[]{:S(2)}, u32[]{:S(2)}) collective-permute-start(bf16[1,8,256]{2,1,0:T(8,128)(2,1)S(1)} %get-tuple-element.109), channel_id=1, source_target_pairs={{0,4},{4,8},{8,12},{1,5},{5,9},{9,13},{2,6},{6,10},{10,14},{3,7},{... | collective-permute-start | bytes 12296 | tf_op jit(solution)/shard_map/ppermute | solution.py:15
  89.9 4.8 %collective-permute-start.3 = (bf16[1,8,256]{2,1,0:T(8,128)(2,1)S(1)}, bf16[1,8,256]{2,1,0:T(8,128)(2,1)S(1)}, u32[]{:S(2)}, u32[]{:S(2)}) collective-permute-start(bf16[1,8,256]{2,1,0:T(8,128)(2,1)S(1)} %get-tuple-element.110), channel_id=1, source_target_pairs={{4,0},{8,4},{12,8},{5,1},{9,5},{13,9},{6,2},{10,6},{14,10},{7,3},{... | collective-permute-start | bytes 12296 | tf_op jit(solution)/shard_map/ppermute | solution.py:18
  94.7 2.6 %collective-permute-start.4 = (bf16[4,1,256]{2,1,0:T(2,128)(2,1)S(1)}, bf16[4,1,256]{2,1,0:T(2,128)(2,1)S(1)}, u32[]{:S(2)}, u32[]{:S(2)}) collective-permute-start(bf16[4,1,256]{2,1,0:T(2,128)(2,1)S(1)} %get-tuple-element.107), channel_id=1, source_target_pairs={{0,1},{1,2},{2,3},{4,5},{5,6},{6,7},{8,9},{9,10},{10,11},{12,13},{... | collective-permute-start | bytes 6152 | tf_op jit(solution)/shard_map/ppermute | solution.py:15
  96.0 5.5 %collective-permute-start.5 = (bf16[4,1,256]{2,1,0:T(2,128)(2,1)S(1)}, bf16[4,1,256]{2,1,0:T(2,128)(2,1)S(1)}, u32[]{:S(2)}, u32[]{:S(2)}) collective-permute-start(bf16[4,1,256]{2,1,0:T(2,128)(2,1)S(1)} %get-tuple-element.108), channel_id=1, source_target_pairs={{1,0},{2,1},{3,2},{5,4},{6,5},{7,6},{9,8},{10,9},{11,10},{13,12},{... | collective-permute-start | bytes 6152 | tf_op jit(solution)/shard_map/ppermute | solution.py:18
  108.6 3.7 %collective-permute-start.6 = (bf16[1,16,256]{2,1,0:T(8,128)(2,1)S(1)}, bf16[1,16,256]{2,1,0:T(8,128)(2,1)S(1)}, u32[]{:S(2)}, u32[]{:S(2)}) collective-permute-start(bf16[1,16,256]{2,1,0:T(8,128)(2,1)S(1)} %get-tuple-element.89), channel_id=1, source_target_pairs={{0,4},{4,8},{8,12},{1,5},{5,9},{9,13},{2,6},{6,10},{10,14},{3,7},{... | collective-permute-start | bytes 24584 | tf_op jit(solution)/shard_map/ppermute | solution.py:15
  109.9 4.8 %collective-permute-start.7 = (bf16[1,16,256]{2,1,0:T(8,128)(2,1)S(1)}, bf16[1,16,256]{2,1,0:T(8,128)(2,1)S(1)}, u32[]{:S(2)}, u32[]{:S(2)}) collective-permute-start(bf16[1,16,256]{2,1,0:T(8,128)(2,1)S(1)} %get-tuple-element.90), channel_id=1, source_target_pairs={{4,0},{8,4},{12,8},{5,1},{9,5},{13,9},{6,2},{10,6},{14,10},{7,3},{... | collective-permute-start | bytes 24584 | tf_op jit(solution)/shard_map/ppermute | solution.py:18
  114.7 2.8 %collective-permute-start.8 = (bf16[6,1,256]{2,1,0:T(2,128)(2,1)S(1)}, bf16[6,1,256]{2,1,0:T(2,128)(2,1)S(1)}, u32[]{:S(2)}, u32[]{:S(2)}) collective-permute-start(bf16[6,1,256]{2,1,0:T(2,128)(2,1)S(1)} %get-tuple-element.81), channel_id=1, source_target_pairs={{0,1},{1,2},{2,3},{4,5},{5,6},{6,7},{8,9},{9,10},{10,11},{12,13},{... | collective-permute-start | bytes 9224 | tf_op jit(solution)/shard_map/ppermute | solution.py:15
  116.0 5.5 %collective-permute-start.9 = (bf16[6,1,256]{2,1,0:T(2,128)(2,1)S(1)}, bf16[6,1,256]{2,1,0:T(2,128)(2,1)S(1)}, u32[]{:S(2)}, u32[]{:S(2)}) collective-permute-start(bf16[6,1,256]{2,1,0:T(2,128)(2,1)S(1)} %get-tuple-element.82), channel_id=1, source_target_pairs={{1,0},{2,1},{3,2},{5,4},{6,5},{7,6},{9,8},{10,9},{11,10},{13,12},{... | collective-permute-start | bytes 9224 | tf_op jit(solution)/shard_map/ppermute | solution.py:18
  123.1 5.5 %collective-permute-start.22 = (bf16[1,16,256]{2,1,0:T(8,128)(2,1)S(1)}, bf16[1,16,256]{2,1,0:T(8,128)(2,1)S(1)}, u32[]{:S(2)}, u32[]{:S(2)}) collective-permute-start(bf16[1,16,256]{2,1,0:T(8,128)(2,1)S(1)} %get-tuple-element.85), channel_id=1, source_target_pairs={{0,4},{4,8},{8,12},{1,5},{5,9},{9,13},{2,6},{6,10},{10,14},{3,7},{... | collective-permute-start | bytes 24584 | tf_op jit(solution)/shard_map/ppermute | solution.py:15
  126.3 3.8 %collective-permute-start.23 = (bf16[1,16,256]{2,1,0:T(8,128)(2,1)S(1)}, bf16[1,16,256]{2,1,0:T(8,128)(2,1)S(1)}, u32[]{:S(2)}, u32[]{:S(2)}) collective-permute-start(bf16[1,16,256]{2,1,0:T(8,128)(2,1)S(1)} %get-tuple-element.86), channel_id=1, source_target_pairs={{4,0},{8,4},{12,8},{5,1},{9,5},{13,9},{6,2},{10,6},{14,10},{7,3},{... | collective-permute-start | bytes 24584 | tf_op jit(solution)/shard_map/ppermute | solution.py:18
  130.0 10.3 %collective-permute-start.24 = (bf16[6,1,256]{2,1,0:T(2,128)(2,1)S(1)}, bf16[6,1,256]{2,1,0:T(2,128)(2,1)S(1)}, u32[]{:S(2)}, u32[]{:S(2)}) collective-permute-start(bf16[6,1,256]{2,1,0:T(2,128)(2,1)S(1)} %get-tuple-element.77), channel_id=1, source_target_pairs={{0,1},{1,2},{2,3},{4,5},{5,6},{6,7},{8,9},{9,10},{10,11},{12,13},{... | collective-permute-start | bytes 9224 | tf_op jit(solution)/shard_map/ppermute | solution.py:15
  133.7 6.7 %collective-permute-start.25 = (bf16[6,1,256]{2,1,0:T(2,128)(2,1)S(1)}, bf16[6,1,256]{2,1,0:T(2,128)(2,1)S(1)}, u32[]{:S(2)}, u32[]{:S(2)}) collective-permute-start(bf16[6,1,256]{2,1,0:T(2,128)(2,1)S(1)} %get-tuple-element.78), channel_id=1, source_target_pairs={{1,0},{2,1},{3,2},{5,4},{6,5},{7,6},{9,8},{10,9},{11,10},{13,12},{... | collective-permute-start | bytes 9224 | tf_op jit(solution)/shard_map/ppermute | solution.py:18
  135.0 7.0 %collective-permute-start.10 = (bf16[1,32,256]{2,1,0:T(8,128)(2,1)S(1)}, bf16[1,32,256]{2,1,0:T(8,128)(2,1)S(1)}, u32[]{:S(2)}, u32[]{:S(2)}) collective-permute-start(bf16[1,32,256]{2,1,0:T(8,128)(2,1)S(1)} %get-tuple-element.65), channel_id=1, source_target_pairs={{0,4},{4,8},{8,12},{1,5},{5,9},{9,13},{2,6},{6,10},{10,14},{3,7},{... | collective-permute-start | bytes 49160 | tf_op jit(solution)/shard_map/ppermute | solution.py:15
  139.1 3.1 %collective-permute-start.11 = (bf16[1,32,256]{2,1,0:T(8,128)(2,1)S(1)}, bf16[1,32,256]{2,1,0:T(8,128)(2,1)S(1)}, u32[]{:S(2)}, u32[]{:S(2)}) collective-permute-start(bf16[1,32,256]{2,1,0:T(8,128)(2,1)S(1)} %get-tuple-element.66), channel_id=1, source_target_pairs={{4,0},{8,4},{12,8},{5,1},{9,5},{13,9},{6,2},{10,6},{14,10},{7,3},{... | collective-permute-start | bytes 49160 | tf_op jit(solution)/shard_map/ppermute | solution.py:18
  142.2 6.1 %collective-permute-start.12 = (bf16[10,1,256]{2,1,0:T(2,128)(2,1)S(1)}, bf16[10,1,256]{2,1,0:T(2,128)(2,1)S(1)}, u32[]{:S(2)}, u32[]{:S(2)}) collective-permute-start(bf16[10,1,256]{2,1,0:T(2,128)(2,1)S(1)} %get-tuple-element.50), channel_id=1, source_target_pairs={{0,1},{1,2},{2,3},{4,5},{5,6},{6,7},{8,9},{9,10},{10,11},{12,13},{... | collective-permute-start | bytes 15368 | tf_op jit(solution)/shard_map/ppermute | solution.py:15
  146.6 5.6 %collective-permute-start.13 = (bf16[10,1,256]{2,1,0:T(2,128)(2,1)S(1)}, bf16[10,1,256]{2,1,0:T(2,128)(2,1)S(1)}, u32[]{:S(2)}, u32[]{:S(2)}) collective-permute-start(bf16[10,1,256]{2,1,0:T(2,128)(2,1)S(1)} %get-tuple-element.51), channel_id=1, source_target_pairs={{1,0},{2,1},{3,2},{5,4},{6,5},{7,6},{9,8},{10,9},{11,10},{13,12},{... | collective-permute-start | bytes 15368 | tf_op jit(solution)/shard_map/ppermute | solution.py:18
  154.8 5.7 %collective-permute-start.18 = (bf16[1,32,256]{2,1,0:T(8,128)(2,1)S(1)}, bf16[1,32,256]{2,1,0:T(8,128)(2,1)S(1)}, u32[]{:S(2)}, u32[]{:S(2)}) collective-permute-start(bf16[1,32,256]{2,1,0:T(8,128)(2,1)S(1)} %get-tuple-element.61), channel_id=1, source_target_pairs={{0,4},{4,8},{8,12},{1,5},{5,9},{9,13},{2,6},{6,10},{10,14},{3,7},{... | collective-permute-start | bytes 49160 | tf_op jit(solution)/shard_map/ppermute | solution.py:15
  157.7 4.3 %collective-permute-start.19 = (bf16[1,32,256]{2,1,0:T(8,128)(2,1)S(1)}, bf16[1,32,256]{2,1,0:T(8,128)(2,1)S(1)}, u32[]{:S(2)}, u32[]{:S(2)}) collective-permute-start(bf16[1,32,256]{2,1,0:T(8,128)(2,1)S(1)} %get-tuple-element.62), channel_id=1, source_target_pairs={{4,0},{8,4},{12,8},{5,1},{9,5},{13,9},{6,2},{10,6},{14,10},{7,3},{... | collective-permute-start | bytes 49160 | tf_op jit(solution)/shard_map/ppermute | solution.py:18
  162.1 9.1 %collective-permute-start.20 = (bf16[10,1,256]{2,1,0:T(2,128)(2,1)S(1)}, bf16[10,1,256]{2,1,0:T(2,128)(2,1)S(1)}, u32[]{:S(2)}, u32[]{:S(2)}) collective-permute-start(bf16[10,1,256]{2,1,0:T(2,128)(2,1)S(1)} %get-tuple-element.46), channel_id=1, source_target_pairs={{0,1},{1,2},{2,3},{4,5},{5,6},{6,7},{8,9},{9,10},{10,11},{12,13},{... | collective-permute-start | bytes 15368 | tf_op jit(solution)/shard_map/ppermute | solution.py:15
  164.4 6.7 %collective-permute-start.21 = (bf16[10,1,256]{2,1,0:T(2,128)(2,1)S(1)}, bf16[10,1,256]{2,1,0:T(2,128)(2,1)S(1)}, u32[]{:S(2)}, u32[]{:S(2)}) collective-permute-start(bf16[10,1,256]{2,1,0:T(2,128)(2,1)S(1)} %get-tuple-element.47), channel_id=1, source_target_pairs={{1,0},{2,1},{3,2},{5,4},{6,5},{7,6},{9,8},{10,9},{11,10},{13,12},{... | collective-permute-start | bytes 15368 | tf_op jit(solution)/shard_map/ppermute | solution.py:18
  165.8 7.6 %collective-permute-start.14 = (bf16[1,64,256]{2,1,0:T(8,128)(2,1)S(1)}, bf16[1,64,256]{2,1,0:T(8,128)(2,1)S(1)}, u32[]{:S(2)}, u32[]{:S(2)}) collective-permute-start(bf16[1,64,256]{2,1,0:T(8,128)(2,1)S(1)} %get-tuple-element.34), channel_id=1, source_target_pairs={{0,4},{4,8},{8,12},{1,5},{5,9},{9,13},{2,6},{6,10},{10,14},{3,7},{... | collective-permute-start | bytes 98312 | tf_op jit(solution)/shard_map/ppermute | solution.py:15
  169.9 3.5 %collective-permute-start.15 = (bf16[1,64,256]{2,1,0:T(8,128)(2,1)S(1)}, bf16[1,64,256]{2,1,0:T(8,128)(2,1)S(1)}, u32[]{:S(2)}, u32[]{:S(2)}) collective-permute-start(bf16[1,64,256]{2,1,0:T(8,128)(2,1)S(1)} %get-tuple-element.35), channel_id=1, source_target_pairs={{4,0},{8,4},{12,8},{5,1},{9,5},{13,9},{6,2},{10,6},{14,10},{7,3},{... | collective-permute-start | bytes 98312 | tf_op jit(solution)/shard_map/ppermute | solution.py:18
  173.4 6.0 %collective-permute-start.16 = (bf16[18,1,256]{2,1,0:T(2,128)(2,1)S(1)}, bf16[18,1,256]{2,1,0:T(2,128)(2,1)S(1)}, u32[]{:S(2)}, u32[]{:S(2)}) collective-permute-start(bf16[18,1,256]{2,1,0:T(2,128)(2,1)S(1)} %get-tuple-element.30), channel_id=1, source_target_pairs={{0,1},{1,2},{2,3},{4,5},{5,6},{6,7},{8,9},{9,10},{10,11},{12,13},{... | collective-permute-start | bytes 27656 | tf_op jit(solution)/shard_map/ppermute | solution.py:15
  177.7 5.7 %collective-permute-start.17 = (bf16[18,1,256]{2,1,0:T(2,128)(2,1)S(1)}, bf16[18,1,256]{2,1,0:T(2,128)(2,1)S(1)}, u32[]{:S(2)}, u32[]{:S(2)}) collective-permute-start(bf16[18,1,256]{2,1,0:T(2,128)(2,1)S(1)} %get-tuple-element.31), channel_id=1, source_target_pairs={{1,0},{2,1},{3,2},{5,4},{6,5},{7,6},{9,8},{10,9},{11,10},{13,12},{... | collective-permute-start | bytes 27656 | tf_op jit(solution)/shard_map/ppermute | solution.py:18
  187.6 4.8 %collective-permute-start.26 = (bf16[1,64,1024]{2,1,0:T(8,128)(2,1)S(1)}, bf16[1,64,1024]{2,1,0:T(8,128)(2,1)S(1)}, u32[]{:S(2)}, u32[]{:S(2)}) collective-permute-start(bf16[1,64,1024]{2,1,0:T(8,128)(2,1)S(1)} %get-tuple-element.20), channel_id=1, source_target_pairs={{0,4},{4,8},{8,12},{1,5},{5,9},{9,13},{2,6},{6,10},{10,14},{3,7},{... | collective-permute-start | bytes 393224 | tf_op jit(solution)/shard_map/ppermute | solution.py:15
  190.3 4.8 %collective-permute-start.27 = (bf16[1,64,1024]{2,1,0:T(8,128)(2,1)S(1)}, bf16[1,64,1024]{2,1,0:T(8,128)(2,1)S(1)}, u32[]{:S(2)}, u32[]{:S(2)}) collective-permute-start(bf16[1,64,1024]{2,1,0:T(8,128)(2,1)S(1)} %get-tuple-element.21), channel_id=1, source_target_pairs={{4,0},{8,4},{12,8},{5,1},{9,5},{13,9},{6,2},{10,6},{14,10},{7,3},{... | collective-permute-start | bytes 393224 | tf_op jit(solution)/shard_map/ppermute | solution.py:18
  195.3 5.5 %collective-permute-start.28 = (bf16[18,1,1024]{2,1,0:T(2,128)(2,1)S(1)}, bf16[18,1,1024]{2,1,0:T(2,128)(2,1)S(1)}, u32[]{:S(2)}, u32[]{:S(2)}) collective-permute-start(bf16[18,1,1024]{2,1,0:T(2,128)(2,1)S(1)} %get-tuple-element.16), channel_id=1, source_target_pairs={{0,1},{1,2},{2,3},{4,5},{5,6},{6,7},{8,9},{9,10},{10,11},{12,13},{... | collective-permute-start | bytes 110600 | tf_op jit(solution)/shard_map/ppermute | solution.py:15
  197.2 6.2 %collective-permute-start.29 = (bf16[18,1,1024]{2,1,0:T(2,128)(2,1)S(1)}, bf16[18,1,1024]{2,1,0:T(2,128)(2,1)S(1)}, u32[]{:S(2)}, u32[]{:S(2)}) collective-permute-start(bf16[18,1,1024]{2,1,0:T(2,128)(2,1)S(1)} %get-tuple-element.17), channel_id=1, source_target_pairs={{1,0},{2,1},{3,2},{5,4},{6,5},{7,6},{9,8},{10,9},{11,10},{13,12},{... | collective-permute-start | bytes 110600 | tf_op jit(solution)/shard_map/ppermute | solution.py:18
  (20 other events, 242.5 us)
Sparse Core Ops, SparseCore 0:
  71.0 16.8 reduce-scatter.6
  90.2 17.3 reduce-scatter.4
where the time goes:
time: 227 us; the launch traced here: 224 us
  starting transfers between devices  61.5 us (27%)
  waiting for transfers between devices  46.3 us (20%)
  matrix products  33.9 us (15%)
  blocking collectives  32.9 us (14%)
  other arithmetic  19.2 us (8%)
  between operations  15.2 us (7%)
  local copies, waits for them, and re-layouts  14.4 us (6%)
    ppermute x15, starting transfers between devices, with_halo(): lax.ppermute(lax.slice_in_dim(block, block.shape[dim] - width, None, axis...  41.7 us
    ppermute x15, waiting for transfers between devices, with_halo(): lax.ppermute(lax.slice_in_dim(block, 0, width, axis=dim), axis, backward)  30.5 us
    ppermute x15, starting transfers between devices, with_halo(): lax.ppermute(lax.slice_in_dim(block, 0, width, axis=dim), axis, backward)  19.8 us
    psum x1, blocking collectives, local(): lax.psum(bin_terms(pooled_split).astype(jnp.bfloat16), 'col')  19.2 us
    dot_general x45, matrix products, taps_sum(): jnp.dot(window, weight[row_tap, col_tap], preferred_element_type=jnp.floa...  13.8 us
    psum x1, blocking collectives, local(): lax.psum(jnp.concatenate(pooled_parts, axis=0).astype(jnp.bfloat16), 'row')  13.7 us
    unnamed x3, waiting for transfers between devices  10.4 us
    concatenate x13, other arithmetic, with_halo(): block = jnp.concatenate([low, block, high], axis=dim)  6.99 us
  transfers between devices with their start and end apart: 32, of which 13 were waited for; matrix products, arithmetic and copies ran while one was open for 18% of the time, Pallas kernels for 0%

commit v1 on v0

v1 whole, which is shorter than its diff:
```python
import functools
import jax
import jax.numpy as jnp
import numpy as np
from jax import lax
from jax.experimental import pallas as pl
from jax.experimental.pallas import tpu as pltpu
from jax.sharding import PartitionSpec as P

bin_sides = (1, 2, 3, 6)
MESH = pl.DeviceIdType.MESH
EDGE = 16
CELLS = 48


def round_up(value, unit):
    return -(-value // unit) * unit


def pool_counts(rows, cols):
    member = np.zeros((len(bin_sides) * CELLS, rows * cols), np.float32)
    scale = np.zeros((len(bin_sides) * CELLS, 1), np.float32)
    for k, b in enumerate(bin_sides):
        for i in range(b):
            for j in range(b):
                r0, r1 = i * rows // b, -(-(i + 1) * rows // b)
                c0, c1 = j * cols // b, -(-(j + 1) * cols // b)
                cell = np.zeros((rows, cols), np.float32)
                cell[r0:r1, c0:c1] = 1.0
                member[k * CELLS + i * b + j] = cell.reshape(-1)
                scale[k * CELLS + i * b + j] = 1.0 / ((r1 - r0) * (c1 - c0))
    return member, scale


def stretch(count, bin_side):
    place = np.arange(count, dtype=np.float32)
    source = np.clip((place + 0.5) * bin_side / count - 0.5, 0.0, bin_side - 1.0)
    return np.maximum(0.0, 1.0 - np.abs(source[:, None] - np.arange(bin_side)[None, :]))


def spread_table(rows, cols, border):
    table = np.zeros((len(bin_sides), rows + 2 * border, cols, CELLS), np.float32)
    for k, b in enumerate(bin_sides):
        both = stretch(rows, b)[:, None, :, None] * stretch(cols, b)[None, :, None, :]
        table[k, border : border + rows, :, : b * b] = both.reshape(rows, cols, b * b)
    return table.reshape(len(bin_sides), (rows + 2 * border) * cols, CELLS)


def pick_table(rows, cols, parts, first, width):
    own = cols // parts
    table = np.zeros((parts, rows, width, rows, cols), np.float32)
    for part in range(parts):
        for j in range(width):
            source = part * own + first + j
            if 0 <= source < cols:
                for r in range(rows):
                    table[part, r, j, r, source] = 1.0
    return table.reshape(parts * rows * width, rows * cols)


def dot(a, b):
    return jnp.dot(a, b, preferred_element_type=jnp.float32)


def front(
    sizes, one, two, three, four, bins, neck, necked, offsets, bin_bias, member, scale, spread,
    pick_top, pick_three,
    f1, f2, t3, top,
    grid, rows3, send3, bin_out, bin_in, sendt, gott, ppm,
    sem_four, sem_row, sem_col, sem_three, sem_bin, sem_top,
):
    count_r, count_c = sizes
    row, col = lax.axis_index("row"), lax.axis_index("col")
    h1, w1, _ = one.shape
    h2, w2, _ = two.shape
    h3, w3, _ = three.shape
    h4, w4, c4 = four.shape
    share = necked.shape[2]
    channels = neck.shape[3]
    wide3 = t3.shape[1]
    wide_t = top.shape[0]
    border = 3

    for frame, block, h, w in ((f1, one, h1, w1), (f2, two, h2, w2)):
        depth = frame.shape[2]
        frame[0:2] = jnp.zeros((2, w + 2 * EDGE, depth), frame.dtype)
        frame[2 + h :] = jnp.zeros((2, w + 2 * EDGE, depth), frame.dtype)
        frame[2 : 2 + h, 0:EDGE] = jnp.zeros((h, EDGE, depth), frame.dtype)
        frame[2 : 2 + h, EDGE + w :] = jnp.zeros((h, EDGE, depth), frame.dtype)
    rows3[0:2] = jnp.zeros((2, w3, three.shape[2]), rows3.dtype)
    rows3[2 + h3 :] = jnp.zeros((2, w3, three.shape[2]), rows3.dtype)
    grid[0:border] = jnp.zeros((border, w4, c4), grid.dtype)
    grid[border + h4 * count_r :] = jnp.zeros((border, w4, c4), grid.dtype)

    barrier = pltpu.get_barrier_semaphore()
    for step in range(1, count_r):
        pl.semaphore_signal(
            barrier, inc=1, device_id={"row": lax.rem(row + step, count_r)}, device_id_type=MESH
        )
    for step in range(1, count_c):
        pl.semaphore_signal(
            barrier, inc=1, device_id={"col": lax.rem(col + step, count_c)}, device_id_type=MESH
        )
    pl.semaphore_wait(barrier, count_r + count_c - 2)

    def remote(source, target, sems, number, where):
        return pltpu.make_async_remote_copy(
            src_ref=source, dst_ref=target, send_sem=sems.at[0, number],
            recv_sem=sems.at[1, number], device_id=where, device_id_type=MESH,
        )

    four_copies = []
    for step in range(1, count_r):
        copy = remote(
            four, grid.at[pl.ds(border + row * h4, h4)], sem_four, step - 1,
            {"row": lax.rem(row + step, count_r)},
        )
        copy.start()
        four_copies.append(copy)
    up_copies, down_copies = [], []
    for number, (block, frame, h, w, left) in enumerate(
        ((three, rows3, h3, w3, 0), (one, f1, h1, w1, EDGE), (two, f2, h2, w2, EDGE))
    ):
        up_copies.append(
            remote(block.at[0:2], frame.at[2 + h : 4 + h, left : left + w], sem_row, number,
                   {"row": row - 1})
        )
        down_copies.append(
            remote(block.at[h - 2 : h], frame.at[0:2, left : left + w], sem_row, 3 + number,
                   {"row": row + 1})
        )

    @pl.when(row > 0)
    def _():
        for copy in up_copies:
            copy.start()

    @pl.when(row < count_r - 1)
    def _():
        for copy in down_copies:
            copy.start()

    grid[pl.ds(border + row * h4, h4)] = four[...]
    f1[2 : 2 + h1, EDGE : EDGE + w1] = one[...]
    f2[2 : 2 + h2, EDGE : EDGE + w2] = two[...]
    rows3[2 : 2 + h3] = three[...]
    for copy in four_copies:
        copy.wait_recv()

    whole = grid[border : border + h4 * count_r].reshape(h4 * count_r * w4, c4)
    pooled = dot(member[...], whole) * scale[...]
    high = pooled.astype(jnp.bfloat16)
    low = (pooled - high.astype(jnp.float32)).astype(jnp.bfloat16)
    for k in range(len(bin_sides)):
        rows = slice(k * CELLS, (k + 1) * CELLS)
        part = (dot(high[rows], bins[k]) + dot(low[rows], bins[k])).astype(jnp.bfloat16)
        for piece in range(channels // share):
            bin_out[k * (channels // share) + piece] = part[:, piece * share : (piece + 1) * share]
    bin_copies = []
    for step in range(1, count_c):
        there = lax.rem(col + step, count_c)
        copy = remote(bin_out.at[there], bin_in.at[col], sem_bin, step - 1, {"col": there})
        copy.start()
        bin_copies.append(copy)
    bin_in[pl.ds(col, 1)] = bin_out[pl.ds(col, 1)]

    @pl.when(row < count_r - 1)
    def _():
        for copy in up_copies:
            copy.wait_recv()

    @pl.when(row > 0)
    def _():
        for copy in down_copies:
            copy.wait_recv()

    left_copies, right_copies = [], []
    for number, (frame, w) in enumerate(((f1, w1), (f2, w2))):
        left_copies.append(
            remote(frame.at[:, EDGE : 2 * EDGE], frame.at[:, EDGE + w :], sem_col, number,
                   {"col": col - 1})
        )
        right_copies.append(
            remote(frame.at[:, w : EDGE + w], frame.at[:, 0:EDGE], sem_col, 2 + number,
                   {"col": col + 1})
        )

    @pl.when(col > 0)
    def _():
        for copy in left_copies:
            copy.start()

    @pl.when(col < count_c - 1)
    def _():
        for copy in right_copies:
            copy.start()

    tall3 = rows3[...].reshape((h3 + 4) * w3, three.shape[2])
    for part in range(count_c):
        send3[part] = dot(
            pick_three[part * wide3 : (part + 1) * wide3], tall3
        ).astype(jnp.bfloat16)
    three_copies = []
    for step in range(1, count_c):
        there = lax.rem(col + step, count_c)
        copy = remote(send3.at[there], t3.at[col], sem_three, step - 1, {"col": there})
        copy.start()
        three_copies.append(copy)
    t3[pl.ds(col, 1)] = send3[pl.ds(col, 1)]

    tall = h4 + 4
    terms = [None] * 3
    for dy in range(3):
        window = grid[pl.ds(row * h4 + dy, tall)].reshape(tall * w4, c4)
        for dx in range(3):
            term = dot(window, neck[dy, dx])
            terms[dx] = term if dy == 0 else terms[dx] + term

    for copy in bin_copies:
        copy.wait_recv()
    total = bin_in[0].astype(jnp.float32)
    for part in range(1, count_c):
        total = total + bin_in[part].astype(jnp.float32)
    binned = jnp.maximum(total + bin_bias[pl.ds(col, 1)].reshape(1, share), 0.0)
    branch = col * share // channels
    table = spread[branch, pl.ds(pl.multiple_of(row * h4 * w4, 8), (tall + 2) * w4), :]
    ppm[...] = (
        jnp.dot(table, binned, precision=lax.Precision.HIGHEST, preferred_element_type=jnp.float32)
        .astype(jnp.bfloat16)
        .reshape(tall + 2, w4, share)
    )
    for dy in range(3):
        window = ppm[dy : dy + tall].reshape(tall * w4, share)
        for dx in range(3):
            terms[dx] = terms[dx] + dot(window, necked[dy, dx])
    place = lax.rem(lax.broadcasted_iota(jnp.int32, (tall * w4, 1), 0), w4)
    partial = (
        terms[1]
        + jnp.where(place > 0, pltpu.roll(terms[0], 1, 0), 0.0)
        + jnp.where(place < w4 - 1, pltpu.roll(terms[2], tall * w4 - 1, 0), 0.0)
    ).astype(jnp.bfloat16)
    for part in range(count_c):
        sendt[part] = dot(pick_top[part * wide_t : (part + 1) * wide_t], partial).astype(
            jnp.bfloat16
        )
    top_copies = []
    for step in range(1, count_c):
        there = lax.rem(col + step, count_c)
        copy = remote(sendt.at[there], gott.at[col], sem_top, step - 1, {"col": there})
        copy.start()
        top_copies.append(copy)
    gott[pl.ds(col, 1)] = sendt[pl.ds(col, 1)]
    for copy in top_copies:
        copy.wait_recv()
    total = gott[0].astype(jnp.float32)
    for part in range(1, count_c):
        total = total + gott[part].astype(jnp.float32)
    top[...] = jnp.maximum(total + offsets[4:5], 0.0).astype(jnp.bfloat16)

    for copy in three_copies:
        copy.wait_recv()

    @pl.when(col < count_c - 1)
    def _():
        for copy in left_copies:
            copy.wait_recv()

    @pl.when(col > 0)
    def _():
        for copy in right_copies:
            copy.wait_recv()

    for copy in four_copies + bin_copies + three_copies + top_copies:
        copy.wait_send()

    @pl.when(row > 0)
    def _():
        for copy in up_copies:
            copy.wait_send()

    @pl.when(row < count_r - 1)
    def _():
        for copy in down_copies:
            copy.wait_send()

    @pl.when(col > 0)
    def _():
        for copy in left_copies:
            copy.wait_send()

    @pl.when(col < count_c - 1)
    def _():
        for copy in right_copies:
            copy.wait_send()


def column_matrix(col, own, first, width, own_from, first_from, width_from, factor, total):
    place = col * own + first + lax.broadcasted_iota(jnp.int32, (width, width_from), 0)
    source = (place.astype(jnp.float32) + 0.5) / factor - 0.5
    source = jnp.clip(source, 0.0, total // factor - 1.0)
    here = col * own_from + first_from + lax.broadcasted_iota(jnp.int32, (width, width_from), 1)
    weight = jnp.maximum(0.0, 1.0 - jnp.abs(source - here.astype(jnp.float32)))
    return jnp.where((place >= 0) & (place < total), weight, 0.0).astype(jnp.bfloat16)


def back(
    sizes, f1, f2, t3, top, lat1, lat2, lat3, smooth, join, offsets, out,
    p3, p2, p1, s3, s2, joint, wide,
):
    count_r, count_c = sizes
    row, col = lax.axis_index("row"), lax.axis_index("col")
    at_top, at_bottom = row == 0, row == count_r - 1
    h1, w1, channels = out.shape
    h2, w2, h3, w3, h4, w4 = h1 // 2, w1 // 2, h1 // 4, w1 // 4, h1 // 8, w1 // 8
    n1, n2, n3 = w1 + 16, w2 + 16, p3.shape[1]
    n4 = top.shape[0] // (h4 + 4)
    pack3 = t3.shape[1] // (h3 + 4)

    def inside(first, width, own):
        place = col * own + first + lax.broadcasted_iota(jnp.int32, (1, width, 1), 1)
        return (place >= 0) & (place < own * count_c)

    def row_inside(t, h):
        if t < 0:
            return jnp.logical_not(at_top)
        if t >= h:
            return jnp.logical_not(at_bottom)
        return None

    def widen(read, matrix, h, border):
        width = matrix.shape[0]
        for r in range(h + 2 * border):
            wide[r, 0:width] = dot(matrix, read(r))

        @pl.when(at_top)
        def _():
            wide[border - 1, 0:width] = wide[border, 0:width]

        @pl.when(at_bottom)
        def _():
            wide[border + h, 0:width] = wide[border + h - 1, 0:width]

    def interpolate(t, factor, border, width):
        source = (t + 0.5) / factor - 0.5
        low = int(np.floor(source))
        weight = float(source - low)
        return (
            wide[border + low, 0:width] * (1.0 - weight)
            + wide[border + low + 1, 0:width] * weight
        )

    def store_row(target, index, value, t, h, lanes=slice(None)):
        keep = row_inside(t, h)
        if keep is not None:
            value = jnp.where(keep, value, 0.0)
        target[index, :, lanes] = value.astype(jnp.bfloat16)

    def taps(read, weight, stride, rows):
        size = rows * stride
        sums = []
        for dx in range(3):
            total = None
            for dy in range(3):
                term = dot(read(dy), weight(dy, dx))
                total = term if total is None else total + term
            sums.append(total)
        return sums[1] + pltpu.roll(sums[0], 1, 0) + pltpu.roll(sums[2], size - 1, 0)

    term = None
    share = t3.shape[2]
    for part in range(count_c):
        piece = dot(t3[part], lat3[part * share : (part + 1) * share])
        term = piece if term is None else term + piece
    term = jnp.maximum(term + offsets[7:8], 0.0).reshape(h3 + 4, pack3, channels)
    term = jnp.concatenate(
        [term, jnp.zeros((h3 + 4, n3 - pack3, channels), jnp.float32)], axis=1
    )
    keep = inside(-4, n3, w3)
    widen(lambda r: top[r * n4 : (r + 1) * n4],
          column_matrix(col, w3, -4, n3, w4, -4, n4, 2, w3 * count_c), h4, 2)
    for t in range(-2, h3 + 2):
        value = jnp.where(keep[0], term[t + 2] + interpolate(t, 2, 2, n3), 0.0)
        store_row(p3, t + 2, value, t, h3)

    term = dot(f2[...].reshape((h2 + 4) * f2.shape[1], f2.shape[2]), lat2[...])
    term = jnp.maximum(term + offsets[6:7], 0.0).reshape(h2 + 4, f2.shape[1], channels)
    keep = inside(-8, n2, w2)
    widen(lambda r: p3[r], column_matrix(col, w2, -8, n2, w3, -4, n3, 2, w2 * count_c), h3, 2)
    for t in range(-2, h2 + 2):
        value = jnp.where(keep[0], term[t + 2, 8 : 8 + n2] + interpolate(t, 2, 2, n2), 0.0)
        store_row(p2, t + 2, value, t, h2)

    keep = inside(-8, n1, w1)
    widen(lambda r: p2[r], column_matrix(col, w1, -8, n1, w2, -8, n2, 2, w1 * count_c), h2, 2)
    for t in range(-2, h1 + 2):
        term = jnp.maximum(dot(f1[t + 2], lat1[...]) + offsets[5:6], 0.0)
        value = jnp.where(keep[0], term[8 : 8 + n1] + interpolate(t, 2, 2, n1), 0.0)
        store_row(p1, t + 2, value, t, h1)

    value = taps(lambda dy: p3[dy : dy + h3 + 2].reshape((h3 + 2) * n3, channels),
                 lambda dy, dx: smooth[2, dy, dx], n3, h3 + 2)
    s3[...] = jnp.maximum(value + offsets[10:11], 0.0).astype(jnp.bfloat16).reshape(s3.shape)
    value = taps(lambda dy: p2[dy : dy + h2 + 2].reshape((h2 + 2) * n2, channels),
                 lambda dy, dx: smooth[1, dy, dx], n2, h2 + 2)
    s2[...] = jnp.maximum(value + offsets[9:10], 0.0).astype(jnp.bfloat16).reshape(s2.shape)

    group = 6
    @pl.loop(0, (h1 + 2) // group)
    def _(block):
        value = taps(
            lambda dy: p1[pl.ds(block * group + dy, group)].reshape(group * n1, channels),
            lambda dy, dx: smooth[0, dy, dx], n1, group,
        )
        value = jnp.maximum(value + offsets[8:9], 0.0).reshape(group, n1, channels)
        value = jnp.where(keep, value, 0.0)
        joint[pl.ds(block * group, group), :, 0:channels] = value.astype(jnp.bfloat16)

    @pl.when(at_top)
    def _():
        joint[0, :, 0:channels] = jnp.zeros((n1, channels), jnp.bfloat16)

    @pl.when(at_bottom)
    def _():
        joint[h1 + 1, :, 0:channels] = jnp.zeros((n1, channels), jnp.bfloat16)

    total1 = w1 * count_c
    for number, (read, matrix, factor, h, border) in enumerate((
        (lambda r: s2[r], column_matrix(col, w1, -8, n1, w2, -8, n2, 2, total1), 2, h2, 1),
        (lambda r: s3[r], column_matrix(col, w1, -8, n1, w3, -4, n3, 4, total1), 4, h3, 1),
        (lambda r: top[r * n4 : (r + 1) * n4],
         column_matrix(col, w1, -8, n1, w4, -4, n4, 8, total1), 8, h4, 2),
    )):
        widen(read, matrix, h, border)
        lanes = slice((number + 1) * channels, (number + 2) * channels)
        for t in range(-1, h1 + 1):
            store_row(joint, t + 1, interpolate(t, factor, border, n1), t, h1, lanes)

    rows = 4
    @pl.loop(0, h1 // rows)
    def _(block):
        value = taps(
            lambda dy: joint[pl.ds(block * rows + dy, rows)].reshape(rows * n1, joint.shape[2]),
            lambda dy, dx: join[dy, dx], n1, rows,
        )
        value = jnp.maximum(value + offsets[11:12], 0.0).reshape(rows, n1, channels)
        out[pl.ds(block * rows, rows)] = value[:, 8 : 8 + w1].astype(jnp.bfloat16)


def local(
    sizes, level_one, level_two, level_three, level_four, bin_weight, neck_feature, neck_pooled,
    lateral_one, lateral_two, lateral_three, smooth_weight, join_weight, biases,
):
    count_r, count_c = sizes
    h1, w1, c1 = level_one.shape
    h2, w2, c2 = level_two.shape
    h3, wide3, c3 = level_three.shape
    h4, wide4, c4 = level_four.shape
    channels = bin_weight.shape[2]
    share = neck_pooled.shape[2]
    w3, w4 = wide3 // count_c, wide4 // count_c
    bf16, f32 = jnp.bfloat16, jnp.float32
    grid_rows = h4 * count_r
    member, scale = pool_counts(grid_rows, wide4)
    spread = spread_table(grid_rows, wide4, 3)
    pack3, pack4 = w3 + 8, w4 + 8
    pick_top = pick_table(h4 + 4, wide4, count_c, -4, pack4)
    pick_three = pick_table(h3 + 4, wide3, count_c, -4, pack3)
    vmem = pl.BlockSpec(memory_space=pltpu.VMEM)
    dma = pltpu.SemaphoreType.DMA
    frames = pl.pallas_call(
        functools.partial(front, sizes),
        out_shape=(
            jax.ShapeDtypeStruct((h1 + 4, w1 + 2 * EDGE, c1), bf16),
            jax.ShapeDtypeStruct((h2 + 4, w2 + 2 * EDGE, c2), bf16),
            jax.ShapeDtypeStruct((count_c, (h3 + 4) * pack3, c3), bf16),
            jax.ShapeDtypeStruct(((h4 + 4) * pack4, channels), bf16),
        ),
        in_specs=[vmem] * 14,
        out_specs=[vmem] * 4,
        scratch_shapes=[
            pltpu.VMEM((grid_rows + 6, wide4, c4), bf16),
            pltpu.VMEM((h3 + 4, wide3, c3), bf16),
            pltpu.VMEM((count_c, (h3 + 4) * pack3, c3), bf16),
            pltpu.VMEM((count_c, CELLS, share), bf16),
            pltpu.VMEM((count_c, CELLS, share), bf16),
            pltpu.VMEM((count_c, (h4 + 4) * pack4, channels), bf16),
            pltpu.VMEM((count_c, (h4 + 4) * pack4, channels), bf16),
            pltpu.VMEM((h4 + 6, wide4, share), bf16),
            dma((2, max(count_r - 1, 1))),
            dma((2, 6)),
            dma((2, 4)),
            dma((2, max(count_c - 1, 1))),
            dma((2, max(count_c - 1, 1))),
            dma((2, max(count_c - 1, 1))),
        ],
        compiler_params=pltpu.CompilerParams(
            collective_id=0, has_side_effects=True, vmem_limit_bytes=48 * 1024 * 1024
        ),
        name="front",
    )(
        level_one, level_two, level_three, level_four, bin_weight, neck_feature, neck_pooled,
        biases, biases[: len(bin_sides)].reshape(-1, share),
        jnp.asarray(member, bf16), jnp.asarray(scale), jnp.asarray(spread),
        jnp.asarray(pick_top, bf16), jnp.asarray(pick_three, bf16),
    )
    n1, n2, n3 = w1 + 16, w2 + 16, round_up(pack3, 16)
    return pl.pallas_call(
        functools.partial(back, sizes),
        out_shape=jax.ShapeDtypeStruct((h1, w1, channels), bf16),
        in_specs=[vmem] * 10,
        out_specs=vmem,
        scratch_shapes=[
            pltpu.VMEM((h3 + 4, n3, channels), bf16),
            pltpu.VMEM((h2 + 4, n2, channels), bf16),
            pltpu.VMEM((h1 + 4, n1, channels), bf16),
            pltpu.VMEM((h3 + 2, n3, channels), bf16),
            pltpu.VMEM((h2 + 2, n2, channels), bf16),
            pltpu.VMEM((h1 + 2, n1, 4 * channels), bf16),
            pltpu.VMEM((h2 + 4, n1, channels), f32),
        ],
        compiler_params=pltpu.CompilerParams(vmem_limit_bytes=56 * 1024 * 1024),
        name="back",
    )(*frames, lateral_one, lateral_two, lateral_three, smooth_weight, join_weight, biases)


def solution(mesh):
    placed = (
        P(("grp", "row"), "col", None),
        P(("grp", "row"), "col", None),
        P(("grp", "row"), None, "col"),
        P(("grp", "row"), None, "col"),
        P(None, "col", None),
        P(None, None, "col", None),
        P(None, None, "col", None),
        P(),
        P(),
        P(),
        P(),
        P(),
        P(),
    )
    sizes = (mesh.shape["row"], mesh.shape["col"])
    return jax.shard_map(
        functools.partial(local, sizes), mesh=mesh, in_specs=placed,
        out_specs=P(("grp", "row"), "col", None), check_vma=False,
    )
```

time: 227 us -> 66.6 us (0.29); the launches traced: 224 us -> 66 us
  starting transfers between devices: 61.5 us -> 0 us
  Pallas kernels: 0 us -> 51.6 us
  waiting for transfers between devices: 46.3 us -> 0 us
  matrix products: 33.9 us -> 0 us
  blocking collectives: 32.9 us -> 0 us
  other arithmetic: 19.2 us -> 0 us
  between operations: 15.2 us -> 0.03 us
    ppermute x30 -> x0, starting transfers between devices: 61.5 us -> none  [the longest x15 41.7 us: with_halo(): lax.ppermute(lax.slice_in_dim(block, block.shape[dim] - width, None, axis...]
    pallas_call x0 -> x2, Pallas kernels: none -> 51.6 us  [the longest x1 34 us: local(): pl.pallas_call(functools.partial(front, sizes), out_shape=(jax.ShapeDtype...]
    dot_general x78 -> x0, matrix products: 33.9 us -> none  [the longest x45 13.8 us: taps_sum(): jnp.dot(window, weight[row_tap, col_tap], preferred_element_type=jnp.floa...]
    psum x2 -> x0, blocking collectives: 32.9 us -> none  [the longest x1 19.2 us: local(): lax.psum(bin_terms(pooled_split).astype(jnp.bfloat16), 'col')]
    ppermute x30 -> x0, waiting for transfers between devices: 30.5 us -> none  [the longest x15 30.5 us: with_halo(): lax.ppermute(lax.slice_in_dim(block, 0, width, axis=dim), axis, backward)]
    unnamed x3 -> x0, waiting for transfers between devices: 10.4 us -> none
    unnamed x45 -> x30, local copies, waits for them, and re-layouts: 4.35 us -> 13.7 us
    concatenate x28 -> x0, other arithmetic: 9.23 us -> none  [the longest x13 6.99 us: with_halo(): block = jnp.concatenate([low, block, high], axis=dim)]
  transfers between devices with their start and end apart: 32 -> 0, of which waited for: 13 -> 0; matrix products, arithmetic and copies ran while one was open for 18% -> 0% of each run, Pallas kernels for 0% -> 0%
where the time goes in v1:
time: 66.6 us; the launch traced here: 66 us
  Pallas kernels  51.6 us (77%)
  local copies, waits for them, and re-layouts  14.4 us (22%)
    pallas_call x1, Pallas kernels, local(): pl.pallas_call(functools.partial(front, sizes), out_shape=(jax.ShapeDtype...  34 us
    pallas_call x1, Pallas kernels, local(): pl.pallas_call(functools.partial(back, sizes), out_shape=jax.ShapeDtypeSt...  17.6 us
    unnamed x30, local copies, waits for them, and re-layouts  13.7 us

profile of v1, /device:TPU:0, one launch (start us, length us, event | category | flops | bytes accessed | tf_op | source)
XLA Modules:
  0.0 66.0 jit_solution(2687690408867376122)
XLA Ops:
  0.0 0.7 %slice.3.bin_bias = f32[4,256]{1,0:T(4,128)S(1)} slice(f32[12,256]{1,0:T(8,128)} %offsets.3), slice={[0:4], [0:256]} | slice | bytes 8192 | tf_op jit(solution)/shard_map/slice | solution.py:502
  0.7 0.0 copy-start.1
  0.7 1.2 %copy-done.1 = f32[4,448,48]{2,1,0:T(8,128)S(1)} copy-done((f32[4,448,48]{2,1,0:T(8,128)S(1)}, f32[4,448,48]{2,1,0:T(8,128)}, u32[]{:S(2)}) %copy-start.1) | copy-done | bytes 344088
  1.9 0.0 copy-start.2
  1.9 1.1 %copy-done.2 = bf16[4,384,256]{2,1,0:T(8,128)(2,1)S(1)} copy-done((bf16[4,384,256]{2,1,0:T(8,128)(2,1)S(1)}, bf16[4,384,256]{2,1,0:T(8,128)(2,1)}, u32[]{:S(2)}) %copy-start.2) | copy-done | bytes 786456
  3.0 0.0 copy-start.3
  3.0 1.1 %copy-done.3 = bf16[768,512]{1,0:T(8,128)(2,1)S(1)} copy-done((bf16[768,512]{1,0:T(8,128)(2,1)S(1)}, bf16[768,512]{1,0:T(8,128)(2,1)}, u32[]{:S(2)}) %copy-start.3) | copy-done | bytes 786456
  4.1 0.0 copy-start.5
  4.1 1.0 %copy-done.5 = bf16[16,64,192]{2,1,0:T(8,128)(2,1)S(1)} copy-done((bf16[16,64,192]{2,1,0:T(8,128)(2,1)S(1)}, bf16[16,64,192]{2,1,0:T(8,128)(2,1)}, u32[]{:S(2)}) %copy-start.5) | copy-done | bytes 393240
  5.2 0.0 copy-start.7
  5.2 0.9 %copy-done.7 = bf16[8,32,384]{2,1,0:T(8,128)(2,1)S(1)} copy-done((bf16[8,32,384]{2,1,0:T(8,128)(2,1)S(1)}, bf16[8,32,384]{2,1,0:T(8,128)(2,1)}, u32[]{:S(2)}) %copy-start.7) | copy-done | bytes 196632
  6.1 0.0 copy-start.8
  6.1 0.9 %copy-done.8 = bf16[384,192]{1,0:T(8,128)(2,1)S(1)} copy-done((bf16[384,192]{1,0:T(8,128)(2,1)S(1)}, bf16[384,192]{1,0:T(8,128)(2,1)}, u32[]{:S(2)}) %copy-start.8) | copy-done | bytes 147480
  7.0 0.0 copy-start.9
  7.0 0.9 %copy-done.9 = bf16[4,64,192]{2,1,0:T(8,128)(2,1)S(1)} copy-done((bf16[4,64,192]{2,1,0:T(8,128)(2,1)S(1)}, bf16[4,64,192]{2,1,0:T(8,128)(2,1)}, u32[]{:S(2)}) %copy-start.9) | copy-done | bytes 98328
  7.9 0.0 copy-start.10
  7.9 0.9 %copy-done.10 = f32[192,1]{1,0:T(8,128)S(1)} copy-done((f32[192,1]{1,0:T(8,128)S(1)}, f32[192,1]{1,0:T(8,128)}, u32[]{:S(2)}) %copy-start.10) | copy-done | bytes 792
  8.8 0.0 copy-start.11
  8.8 0.9 %copy-done.11 = bf16[192,256]{1,0:T(8,128)(2,1)S(1)} copy-done((bf16[192,256]{1,0:T(8,128)(2,1)S(1)}, bf16[192,256]{1,0:T(8,128)(2,1)}, u32[]{:S(2)}) %copy-start.11) | copy-done | bytes 98328
  9.7 0.0 copy-start.12
  9.7 0.7 %copy-done.12 = f32[12,256]{1,0:T(8,128)S(1)} copy-done((f32[12,256]{1,0:T(8,128)S(1)}, f32[12,256]{1,0:T(8,128)}, u32[]{:S(2)}) %copy-start.12) | copy-done | bytes 12312
  10.5 0.0 copy-start.13
  10.5 0.8 %copy-done.13 = bf16[2,32,384]{2,1,0:T(8,128)(2,1)S(1)} copy-done((bf16[2,32,384]{2,1,0:T(8,128)(2,1)S(1)}, bf16[2,32,384]{2,1,0:T(8,128)(2,1)}, u32[]{:S(2)}) %copy-start.13) | copy-done | bytes 49176
  11.2 34.0 %front.1 = (bf16[20,96,192]{2,1,0:T(8,128)(2,1)S(1)}, bf16[12,64,384]{2,1,0:T(8,128)(2,1)S(1)}, bf16[4,192,192]{2,1,0:T(8,128)(2,1)S(1)}, bf16[96,256]{1,0:T(8,128)(2,1)S(1)}) custom-call(bf16[16,64,192]{2,1,0:T(8,128)(2,1)S(1)} %copy-done.5, bf16[8,32,384]{2,1,0:T(8,128)(2,1)S(1)} %copy-done.7, bf16[4,64,192]{2,1,0:T(8,128)(2,1)S(1)} %copy-done.9, ...), custom_call_target="tpu_custom_call" | custom-call | tf_op jit(solution)/shard_map/front/pallas_call | solution.py:470
  45.3 0.0 copy-start
  45.3 0.9 %copy-done = bf16[20,96,192]{2,1,0:T(8,128)(2,1)} copy-done((bf16[20,96,192]{2,1,0:T(8,128)(2,1)}, bf16[20,96,192]{2,1,0:T(8,128)(2,1)S(1)}, u32[]{:S(2)}) %copy-start) | copy-done | bytes 737304
  46.2 0.0 copy-start.4
  46.2 0.9 %copy-done.4 = bf16[12,64,384]{2,1,0:T(8,128)(2,1)} copy-done((bf16[12,64,384]{2,1,0:T(8,128)(2,1)}, bf16[12,64,384]{2,1,0:T(8,128)(2,1)S(1)}, u32[]{:S(2)}) %copy-start.4) | copy-done | bytes 589848
  47.1 0.0 copy-start.6
  47.1 0.7 %copy-done.6 = bf16[4,192,192]{2,1,0:T(8,128)(2,1)} copy-done((bf16[4,192,192]{2,1,0:T(8,128)(2,1)}, bf16[4,192,192]{2,1,0:T(8,128)(2,1)S(1)}, u32[]{:S(2)}) %copy-start.6) | copy-done | bytes 294936
  47.8 0.6 copy-done.14
  48.4 17.6 %back.1 = bf16[16,64,256]{2,1,0:T(8,128)(2,1)} custom-call(bf16[20,96,192]{2,1,0:T(8,128)(2,1)} %copy-done, bf16[12,64,384]{2,1,0:T(8,128)(2,1)} %copy-done.4, bf16[4,192,192]{2,1,0:T(8,128)(2,1)} %copy-done.6, bf16[96,256]{1,0:T(8,128)(2,1)} %copy-done.14, bf16[192,256]{1,0:T(8,128)(2,1)} %lat1.1, bf16[384,256]{1,0:T(8,128)(2,1)} %lat2.1, ...), custom_call_target="tpu_custom_call" | custom-call | tf_op jit(solution)/shard_map/back/pallas_call | solution.py:507
  (1 shorter events, 0.0 us)
Async XLA Ops:
  0.7 1.2 %copy-start.1 = (f32[4,448,48]{2,1,0:T(8,128)S(1)}, f32[4,448,48]{2,1,0:T(8,128)}, u32[]{:S(2)}) copy-start(f32[4,448,48]{2,1,0:T(8,128)} %constant.12.clone.spread) | copy-start | bytes 1032196
  1.9 1.1 %copy-start.2 = (bf16[4,384,256]{2,1,0:T(8,128)(2,1)S(1)}, bf16[4,384,256]{2,1,0:T(8,128)(2,1)}, u32[]{:S(2)}) copy-start(bf16[4,384,256]{2,1,0:T(8,128)(2,1)} %bins.1) | copy-start | bytes 2359300
  3.0 1.1 %copy-start.3 = (bf16[768,512]{1,0:T(8,128)(2,1)S(1)}, bf16[768,512]{1,0:T(8,128)(2,1)}, u32[]{:S(2)}) copy-start(bf16[768,512]{1,0:T(8,128)(2,1)} %constant.14.clone.pick_three) | copy-start | bytes 2359300
  4.1 1.0 %copy-start.5 = (bf16[16,64,192]{2,1,0:T(8,128)(2,1)S(1)}, bf16[16,64,192]{2,1,0:T(8,128)(2,1)}, u32[]{:S(2)}) copy-start(bf16[16,64,192]{2,1,0:T(8,128)(2,1)} %one.1) | copy-start | bytes 1179652
  5.2 0.9 %copy-start.7 = (bf16[8,32,384]{2,1,0:T(8,128)(2,1)S(1)}, bf16[8,32,384]{2,1,0:T(8,128)(2,1)}, u32[]{:S(2)}) copy-start(bf16[8,32,384]{2,1,0:T(8,128)(2,1)} %two.1) | copy-start | bytes 589828
  6.1 0.9 %copy-start.8 = (bf16[384,192]{1,0:T(8,128)(2,1)S(1)}, bf16[384,192]{1,0:T(8,128)(2,1)}, u32[]{:S(2)}) copy-start(bf16[384,192]{1,0:T(8,128)(2,1)} %constant.13.clone.pick_top) | copy-start | bytes 442372
  7.0 0.9 %copy-start.9 = (bf16[4,64,192]{2,1,0:T(8,128)(2,1)S(1)}, bf16[4,64,192]{2,1,0:T(8,128)(2,1)}, u32[]{:S(2)}) copy-start(bf16[4,64,192]{2,1,0:T(8,128)(2,1)} %three.1) | copy-start | bytes 294916
  7.9 0.9 %copy-start.10 = (f32[192,1]{1,0:T(8,128)S(1)}, f32[192,1]{1,0:T(8,128)}, u32[]{:S(2)}) copy-start(f32[192,1]{1,0:T(8,128)} %constant.11.clone.scale) | copy-start | bytes 2308
  8.8 0.9 %copy-start.11 = (bf16[192,256]{1,0:T(8,128)(2,1)S(1)}, bf16[192,256]{1,0:T(8,128)(2,1)}, u32[]{:S(2)}) copy-start(bf16[192,256]{1,0:T(8,128)(2,1)} %constant.10.clone.member) | copy-start | bytes 294916
  9.7 0.7 %copy-start.12 = (f32[12,256]{1,0:T(8,128)S(1)}, f32[12,256]{1,0:T(8,128)}, u32[]{:S(2)}) copy-start(f32[12,256]{1,0:T(8,128)} %offsets.3) | copy-start | bytes 36868
  10.5 0.8 %copy-start.13 = (bf16[2,32,384]{2,1,0:T(8,128)(2,1)S(1)}, bf16[2,32,384]{2,1,0:T(8,128)(2,1)}, u32[]{:S(2)}) copy-start(bf16[2,32,384]{2,1,0:T(8,128)(2,1)} %four.1) | copy-start | bytes 147460
  45.3 0.9 %copy-start = (bf16[20,96,192]{2,1,0:T(8,128)(2,1)}, bf16[20,96,192]{2,1,0:T(8,128)(2,1)S(1)}, u32[]{:S(2)}) copy-start(bf16[20,96,192]{2,1,0:T(8,128)(2,1)S(1)} %get-tuple-element.9.f1) | copy-start | bytes 2211844
  46.2 0.9 %copy-start.4 = (bf16[12,64,384]{2,1,0:T(8,128)(2,1)}, bf16[12,64,384]{2,1,0:T(8,128)(2,1)S(1)}, u32[]{:S(2)}) copy-start(bf16[12,64,384]{2,1,0:T(8,128)(2,1)S(1)} %get-tuple-element.10.f2) | copy-start | bytes 1769476
  47.1 0.7 %copy-start.6 = (bf16[4,192,192]{2,1,0:T(8,128)(2,1)}, bf16[4,192,192]{2,1,0:T(8,128)(2,1)S(1)}, u32[]{:S(2)}) copy-start(bf16[4,192,192]{2,1,0:T(8,128)(2,1)S(1)} %get-tuple-element.11.t3) | copy-start | bytes 884740
  47.8 0.6 copy-start.14

commit v2 on v1

--- a/solution.py
+++ b/solution.py
@@ -62,33 +62,66 @@
     return jnp.dot(a, b, preferred_element_type=jnp.float32)
 
 
+def column_pick(height, count, base, flip):
+    shape = (height * EDGE, count) if flip else (count, height * EDGE)
+    packed = lax.broadcasted_iota(jnp.int32, shape, 1 if flip else 0)
+    place = lax.broadcasted_iota(jnp.int32, shape, 0 if flip else 1)
+    hit = place == lax.div(packed, 2) * EDGE + base + lax.rem(packed, 2)
+    return jnp.where(hit, 1.0, 0.0).astype(jnp.bfloat16)
+
+
 def front(
-    sizes, one, two, three, four, bins, neck, necked, offsets, bin_bias, member, scale, spread,
-    pick_top, pick_three,
+    sizes, one_h, two_h, three_h, four_h, bins_h, neck_h, necked_h, offsets_h, member_h, scale_h,
+    spread_h, pick_top_h, pick_three_h,
     f1, f2, t3, top,
-    grid, rows3, send3, bin_out, bin_in, sendt, gott, ppm,
-    sem_four, sem_row, sem_col, sem_three, sem_bin, sem_top,
+    three, bins, neck, necked, offsets, member, scale, table, pick_top, pick_three,
+    grid, send3, bin_out, bin_in, sendt, gott, ppm, out1, in1, out2, in2,
+    sem_local, sem_four, sem_row, sem_col, sem_three, sem_bin, sem_top,
 ):
     count_r, count_c = sizes
     row, col = lax.axis_index("row"), lax.axis_index("col")
-    h1, w1, _ = one.shape
-    h2, w2, _ = two.shape
+    h1, w1, _ = one_h.shape
+    h2, w2, _ = two_h.shape
     h3, w3, _ = three.shape
-    h4, w4, c4 = four.shape
+    h4, w4, c4 = four_h.shape
     share = necked.shape[2]
     channels = neck.shape[3]
-    wide3 = t3.shape[1]
+    packed_row = t3.shape[1] // (h3 + 4)
+    halo3, own3 = 2 * packed_row, h3 * packed_row
     wide_t = top.shape[0]
     border = 3
-
-    for frame, block, h, w in ((f1, one, h1, w1), (f2, two, h2, w2)):
-        depth = frame.shape[2]
-        frame[0:2] = jnp.zeros((2, w + 2 * EDGE, depth), frame.dtype)
-        frame[2 + h :] = jnp.zeros((2, w + 2 * EDGE, depth), frame.dtype)
-        frame[2 : 2 + h, 0:EDGE] = jnp.zeros((h, EDGE, depth), frame.dtype)
-        frame[2 : 2 + h, EDGE + w :] = jnp.zeros((h, EDGE, depth), frame.dtype)
-    rows3[0:2] = jnp.zeros((2, w3, three.shape[2]), rows3.dtype)
-    rows3[2 + h3 :] = jnp.zeros((2, w3, three.shape[2]), rows3.dtype)
+    tall = h4 + 4
+    branch = col * share // channels
+
+    def fetch(source, target, number):
+        copy = pltpu.make_async_copy(source, target, sem_local.at[number])
+        copy.start()
+        return copy
+
+    get_three = [fetch(three_h, three, 0), fetch(pick_three_h, pick_three, 1)]
+    get_four = [
+        fetch(four_h, grid.at[pl.ds(border + row * h4, h4)], 2), fetch(member_h, member, 3),
+        fetch(scale_h, scale, 4), fetch(bins_h, bins, 5),
+    ]
+    get_one = [
+        fetch(one_h, f1.at[2 : 2 + h1, EDGE : EDGE + w1], 6),
+        fetch(two_h, f2.at[2 : 2 + h2, EDGE : EDGE + w2], 7),
+    ]
+    get_neck = [fetch(neck_h, neck, 8)]
+    get_rest = [
+        fetch(spread_h.at[branch, pl.ds(row * h4 * w4, (tall + 2) * w4)], table, 9),
+        fetch(offsets_h, offsets, 10), fetch(necked_h, necked, 11), fetch(pick_top_h, pick_top, 12),
+    ]
+
+    for frame, h in ((f1, h1), (f2, h2)):
+        rim = jnp.zeros((2, frame.shape[1], frame.shape[2]), frame.dtype)
+        frame[0:2] = rim
+        frame[2 + h :] = rim
+    in1[...] = jnp.zeros(in1.shape, in1.dtype)
+    in2[...] = jnp.zeros(in2.shape, in2.dtype)
+    rim = jnp.zeros((count_c, halo3, t3.shape[2]), t3.dtype)
+    t3[:, 0:halo3] = rim
+    t3[:, halo3 + own3 :] = rim
     grid[0:border] = jnp.zeros((border, w4, c4), grid.dtype)
     grid[border + h4 * count_r :] = jnp.zeros((border, w4, c4), grid.dtype)
 
@@ -109,53 +142,65 @@
             recv_sem=sems.at[1, number], device_id=where, device_id_type=MESH,
         )
 
+    def when_each(condition, copies, act):
+        @pl.when(condition)
+        def _():
+            for copy in copies:
+                getattr(copy, act)()
+
+    has_up, has_down = row > 0, row < count_r - 1
+    has_left, has_right = col > 0, col < count_c - 1
+
     four_copies = []
     for step in range(1, count_r):
         copy = remote(
-            four, grid.at[pl.ds(border + row * h4, h4)], sem_four, step - 1,
+            four_h, grid.at[pl.ds(border + row * h4, h4)], sem_four, step - 1,
             {"row": lax.rem(row + step, count_r)},
         )
         copy.start()
         four_copies.append(copy)
+    for copy in get_three:
+        copy.wait()
+    tall3 = three[...].reshape(h3 * w3, three.shape[2])
+    three_copies = []
+    for part in range(count_c):
+        send3[part] = dot(pick_three[part * own3 : (part + 1) * own3], tall3).astype(jnp.bfloat16)
+    for step in range(1, count_c):
+        there = lax.rem(col + step, count_c)
+        copy = remote(
+            send3.at[there], t3.at[col, halo3 : halo3 + own3], sem_three, step - 1, {"col": there}
+        )
+        copy.start()
+        three_copies.append(copy)
+    t3[pl.ds(col, 1), halo3 : halo3 + own3] = send3[pl.ds(col, 1)]
+
     up_copies, down_copies = [], []
-    for number, (block, frame, h, w, left) in enumerate(
-        ((three, rows3, h3, w3, 0), (one, f1, h1, w1, EDGE), (two, f2, h2, w2, EDGE))
-    ):
+    for number, (block, frame, h, w) in enumerate(((one_h, f1, h1, w1), (two_h, f2, h2, w2))):
         up_copies.append(
-            remote(block.at[0:2], frame.at[2 + h : 4 + h, left : left + w], sem_row, number,
+            remote(block.at[0:2], frame.at[2 + h : 4 + h, EDGE : EDGE + w], sem_row, number,
                    {"row": row - 1})
         )
         down_copies.append(
-            remote(block.at[h - 2 : h], frame.at[0:2, left : left + w], sem_row, 3 + number,
+            remote(block.at[h - 2 : h], frame.at[0:2, EDGE : EDGE + w], sem_row, 2 + number,
                    {"row": row + 1})
         )
-
-    @pl.when(row > 0)
-    def _():
-        for copy in up_copies:
-            copy.start()
-
-    @pl.when(row < count_r - 1)
-    def _():
-        for copy in down_copies:
-            copy.start()
-
-    grid[pl.ds(border + row * h4, h4)] = four[...]
-    f1[2 : 2 + h1, EDGE : EDGE + w1] = one[...]
-    f2[2 : 2 + h2, EDGE : EDGE + w2] = two[...]
-    rows3[2 : 2 + h3] = three[...]
+    when_each(has_up, up_copies, "start")
+    when_each(has_down, down_copies, "start")
+
+    for copy in get_four:
+        copy.wait()
     for copy in four_copies:
         copy.wait_recv()
-
     whole = grid[border : border + h4 * count_r].reshape(h4 * count_r * w4, c4)
     pooled = dot(member[...], whole) * scale[...]
     high = pooled.astype(jnp.bfloat16)
     low = (pooled - high.astype(jnp.float32)).astype(jnp.bfloat16)
+    pieces = channels // share
     for k in range(len(bin_sides)):
         rows = slice(k * CELLS, (k + 1) * CELLS)
         part = (dot(high[rows], bins[k]) + dot(low[rows], bins[k])).astype(jnp.bfloat16)
-        for piece in range(channels // share):
-            bin_out[k * (channels // share) + piece] = part[:, piece * share : (piece + 1) * share]
+        for piece in range(pieces):
+            bin_out[k * pieces + piece] = part[:, piece * share : (piece + 1) * share]
     bin_copies = []
     for step in range(1, count_c):
         there = lax.rem(col + step, count_c)
@@ -164,51 +209,8 @@
         bin_copies.append(copy)
     bin_in[pl.ds(col, 1)] = bin_out[pl.ds(col, 1)]
 
-    @pl.when(row < count_r - 1)
-    def _():
-        for copy in up_copies:
-            copy.wait_recv()
-
-    @pl.when(row > 0)
-    def _():
-        for copy in down_copies:
-            copy.wait_recv()
-
-    left_copies, right_copies = [], []
-    for number, (frame, w) in enumerate(((f1, w1), (f2, w2))):
-        left_copies.append(
-            remote(frame.at[:, EDGE : 2 * EDGE], frame.at[:, EDGE + w :], sem_col, number,
-                   {"col": col - 1})
-        )
-        right_copies.append(
-            remote(frame.at[:, w : EDGE + w], frame.at[:, 0:EDGE], sem_col, 2 + number,
-                   {"col": col + 1})
-        )
-
-    @pl.when(col > 0)
-    def _():
-        for copy in left_copies:
-            copy.start()
-
-    @pl.when(col < count_c - 1)
-    def _():
-        for copy in right_copies:
-            copy.start()
-
-    tall3 = rows3[...].reshape((h3 + 4) * w3, three.shape[2])
-    for part in range(count_c):
-        send3[part] = dot(
-            pick_three[part * wide3 : (part + 1) * wide3], tall3
-        ).astype(jnp.bfloat16)
-    three_copies = []
-    for step in range(1, count_c):
-        there = lax.rem(col + step, count_c)
-        copy = remote(send3.at[there], t3.at[col], sem_three, step - 1, {"col": there})
-        copy.start()
-        three_copies.append(copy)
-    t3[pl.ds(col, 1)] = send3[pl.ds(col, 1)]
-
-    tall = h4 + 4
+    for copy in get_neck:
+        copy.wait()
     terms = [None] * 3
     for dy in range(3):
         window = grid[pl.ds(row * h4 + dy, tall)].reshape(tall * w4, c4)
@@ -216,16 +218,24 @@
             term = dot(window, neck[dy, dx])
             terms[dx] = term if dy == 0 else terms[dx] + term
 
+    for copy in get_rest:
+        copy.wait()
     for copy in bin_copies:
         copy.wait_recv()
     total = bin_in[0].astype(jnp.float32)
     for part in range(1, count_c):
         total = total + bin_in[part].astype(jnp.float32)
-    binned = jnp.maximum(total + bin_bias[pl.ds(col, 1)].reshape(1, share), 0.0)
-    branch = col * share // channels
-    table = spread[branch, pl.ds(pl.multiple_of(row * h4 * w4, 8), (tall + 2) * w4), :]
+    line = offsets[pl.ds(branch, 1)]
+    shift = line[:, 0:share]
+    for piece in range(1, pieces):
+        shift = jnp.where(
+            lax.rem(col, pieces) == piece, line[:, piece * share : (piece + 1) * share], shift
+        )
+    binned = jnp.maximum(total + shift, 0.0)
     ppm[...] = (
-        jnp.dot(table, binned, precision=lax.Precision.HIGHEST, preferred_element_type=jnp.float32)
+        jnp.dot(
+            table[...], binned, precision=lax.Precision.HIGHEST, preferred_element_type=jnp.float32
+        )
         .astype(jnp.bfloat16)
         .reshape(tall + 2, w4, share)
     )
@@ -250,6 +260,36 @@
         copy.start()
         top_copies.append(copy)
     gott[pl.ds(col, 1)] = sendt[pl.ds(col, 1)]
+
+    for copy in three_copies:
+        copy.wait_recv()
+    up3 = remote(t3.at[:, halo3 : 2 * halo3], t3.at[:, halo3 + own3 :], sem_row, 4,
+                 {"row": row - 1})
+    down3 = remote(t3.at[:, own3 : own3 + halo3], t3.at[:, 0:halo3], sem_row, 5, {"row": row + 1})
+    when_each(has_up, [up3], "start")
+    when_each(has_down, [down3], "start")
+    for copy in get_one:
+        copy.wait()
+    when_each(has_down, up_copies, "wait_recv")
+    when_each(has_up, down_copies, "wait_recv")
+    left_copies, right_copies = [], []
+    for number, (frame, h, w, outgoing, incoming) in enumerate(
+        ((f1, h1 + 4, w1, out1, in1), (f2, h2 + 4, w2, out2, in2))
+    ):
+        count, depth = outgoing.shape[1:]
+        block = frame[:, EDGE : 2 * EDGE].reshape(h * EDGE, depth)
+        outgoing[0] = dot(column_pick(h, count, 0, False), block).astype(jnp.bfloat16)
+        block = frame[:, w : EDGE + w].reshape(h * EDGE, depth)
+        outgoing[1] = dot(column_pick(h, count, EDGE - 2, False), block).astype(jnp.bfloat16)
+        left_copies.append(
+            remote(outgoing.at[0], incoming.at[1], sem_col, number, {"col": col - 1})
+        )
+        right_copies.append(
+            remote(outgoing.at[1], incoming.at[0], sem_col, 2 + number, {"col": col + 1})
+        )
+    when_each(has_left, left_copies, "start")
+    when_each(has_right, right_copies, "start")
+
     for copy in top_copies:
         copy.wait_recv()
     total = gott[0].astype(jnp.float32)
@@ -257,41 +297,23 @@
         total = total + gott[part].astype(jnp.float32)
     top[...] = jnp.maximum(total + offsets[4:5], 0.0).astype(jnp.bfloat16)
 
-    for copy in three_copies:
-        copy.wait_recv()
-
-    @pl.when(col < count_c - 1)
-    def _():
-        for copy in left_copies:
-            copy.wait_recv()
-
-    @pl.when(col > 0)
-    def _():
-        for copy in right_copies:
-            copy.wait_recv()
+    when_each(has_right, left_copies, "wait_recv")
+    when_each(has_left, right_copies, "wait_recv")
+    for frame, h, w, incoming in ((f1, h1 + 4, w1, in1), (f2, h2 + 4, w2, in2)):
+        count, depth = incoming.shape[1:]
+        value = dot(column_pick(h, count, EDGE - 2, True), incoming[0])
+        frame[:, 0:EDGE] = value.astype(jnp.bfloat16).reshape(h, EDGE, depth)
+        value = dot(column_pick(h, count, 0, True), incoming[1])
+        frame[:, EDGE + w :] = value.astype(jnp.bfloat16).reshape(h, EDGE, depth)
+    when_each(has_down, [up3], "wait_recv")
+    when_each(has_up, [down3], "wait_recv")
 
     for copy in four_copies + bin_copies + three_copies + top_copies:
         copy.wait_send()
-
-    @pl.when(row > 0)
-    def _():
-        for copy in up_copies:
-            copy.wait_send()
-
-    @pl.when(row < count_r - 1)
-    def _():
-        for copy in down_copies:
-            copy.wait_send()
-
-    @pl.when(col > 0)
-    def _():
-        for copy in left_copies:
-            copy.wait_send()
-
-    @pl.when(col < count_c - 1)
-    def _():
-        for copy in right_copies:
-            copy.wait_send()
+    when_each(has_up, up_copies + [up3], "wait_send")
+    when_each(has_down, down_copies + [down3], "wait_send")
+    when_each(has_left, left_copies, "wait_send")
+    when_each(has_right, right_copies, "wait_send")
 
 
 def column_matrix(col, own, first, width, own_from, first_from, width_from, factor, total):
@@ -304,9 +326,17 @@
 
 
 def back(
-    sizes, f1, f2, t3, top, lat1, lat2, lat3, smooth, join, offsets, out,
-    p3, p2, p1, s3, s2, joint, wide,
+    sizes, f1_h, f2_h, t3_h, top_h, lat1_h, lat2_h, lat3_h, smooth_h, join_h, offsets_h, out,
+    f1, f2, t3, top, lat1, lat2, lat3, smooth, join, offsets, p3, p2, p1, s3, s2, joint, wide, sems,
 ):
+    fetches = []
+    for source, target in (
+        (t3_h, t3), (lat3_h, lat3), (offsets_h, offsets), (top_h, top), (f2_h, f2), (lat2_h, lat2),
+        (f1_h, f1), (lat1_h, lat1), (smooth_h, smooth), (join_h, join),
+    ):
+        copy = pltpu.make_async_copy(source, target, sems.at[len(fetches)])
+        copy.start()
+        fetches.append(copy)
     count_r, count_c = sizes
     row, col = lax.axis_index("row"), lax.axis_index("col")
     at_top, at_bottom = row == 0, row == count_r - 1
@@ -366,6 +396,8 @@
             sums.append(total)
         return sums[1] + pltpu.roll(sums[0], 1, 0) + pltpu.roll(sums[2], size - 1, 0)
 
+    for copy in fetches[0:4]:
+        copy.wait()
     term = None
     share = t3.shape[2]
     for part in range(count_c):
@@ -382,6 +414,8 @@
         value = jnp.where(keep[0], term[t + 2] + interpolate(t, 2, 2, n3), 0.0)
         store_row(p3, t + 2, value, t, h3)
 
+    for copy in fetches[4:6]:
+        copy.wait()
     term = dot(f2[...].reshape((h2 + 4) * f2.shape[1], f2.shape[2]), lat2[...])
     term = jnp.maximum(term + offsets[6:7], 0.0).reshape(h2 + 4, f2.shape[1], channels)
     keep = inside(-8, n2, w2)
@@ -390,6 +424,8 @@
         value = jnp.where(keep[0], term[t + 2, 8 : 8 + n2] + interpolate(t, 2, 2, n2), 0.0)
         store_row(p2, t + 2, value, t, h2)
 
+    for copy in fetches[6:8]:
+        copy.wait()
     keep = inside(-8, n1, w1)
     widen(lambda r: p2[r], column_matrix(col, w1, -8, n1, w2, -8, n2, 2, w1 * count_c), h2, 2)
     for t in range(-2, h1 + 2):
@@ -397,6 +433,7 @@
         value = jnp.where(keep[0], term[8 : 8 + n1] + interpolate(t, 2, 2, n1), 0.0)
         store_row(p1, t + 2, value, t, h1)
 
+    fetches[8].wait()
     value = taps(lambda dy: p3[dy : dy + h3 + 2].reshape((h3 + 2) * n3, channels),
                  lambda dy, dx: smooth[2, dy, dx], n3, h3 + 2)
     s3[...] = jnp.maximum(value + offsets[10:11], 0.0).astype(jnp.bfloat16).reshape(s3.shape)
@@ -435,6 +472,7 @@
         for t in range(-1, h1 + 1):
             store_row(joint, t + 1, interpolate(t, factor, border, n1), t, h1, lanes)
 
+    fetches[9].wait()
     rows = 4
     @pl.loop(0, h1 // rows)
     def _(block):
@@ -464,9 +502,12 @@
     spread = spread_table(grid_rows, wide4, 3)
     pack3, pack4 = w3 + 8, w4 + 8
     pick_top = pick_table(h4 + 4, wide4, count_c, -4, pack4)
-    pick_three = pick_table(h3 + 4, wide3, count_c, -4, pack3)
+    pick_three = pick_table(h3, wide3, count_c, -4, pack3)
     vmem = pl.BlockSpec(memory_space=pltpu.VMEM)
+    hbm = pl.BlockSpec(memory_space=pltpu.HBM)
     dma = pltpu.SemaphoreType.DMA
+    steps_r, steps_c = max(count_r - 1, 1), max(count_c - 1, 1)
+    column1, column2 = round_up(2 * (h1 + 4), 16), round_up(2 * (h2 + 4), 16)
     frames = pl.pallas_call(
         functools.partial(front, sizes),
         out_shape=(
@@ -475,41 +516,60 @@
             jax.ShapeDtypeStruct((count_c, (h3 + 4) * pack3, c3), bf16),
             jax.ShapeDtypeStruct(((h4 + 4) * pack4, channels), bf16),
         ),
-        in_specs=[vmem] * 14,
+        in_specs=[hbm] * 13,
         out_specs=[vmem] * 4,
         scratch_shapes=[
+            pltpu.VMEM(level_three.shape, bf16),
+            pltpu.VMEM(bin_weight.shape, bf16),
+            pltpu.VMEM(neck_feature.shape, bf16),
+            pltpu.VMEM(neck_pooled.shape, bf16),
+            pltpu.VMEM(biases.shape, f32),
+            pltpu.VMEM(member.shape, bf16),
+            pltpu.VMEM(scale.shape, f32),
+            pltpu.VMEM(((h4 + 6) * wide4, CELLS), f32),
+            pltpu.VMEM(pick_top.shape, bf16),
+            pltpu.VMEM(pick_three.shape, bf16),
             pltpu.VMEM((grid_rows + 6, wide4, c4), bf16),
-            pltpu.VMEM((h3 + 4, wide3, c3), bf16),
-            pltpu.VMEM((count_c, (h3 + 4) * pack3, c3), bf16),
+            pltpu.VMEM((count_c, h3 * pack3, c3), bf16),
             pltpu.VMEM((count_c, CELLS, share), bf16),
             pltpu.VMEM((count_c, CELLS, share), bf16),
             pltpu.VMEM((count_c, (h4 + 4) * pack4, channels), bf16),
             pltpu.VMEM((count_c, (h4 + 4) * pack4, channels), bf16),
             pltpu.VMEM((h4 + 6, wide4, share), bf16),
-            dma((2, max(count_r - 1, 1))),
+            pltpu.VMEM((2, column1, c1), bf16),
+            pltpu.VMEM((2, column1, c1), bf16),
+            pltpu.VMEM((2, column2, c2), bf16),
+            pltpu.VMEM((2, column2, c2), bf16),
+            dma((13,)),
+            dma((2, steps_r)),
             dma((2, 6)),
             dma((2, 4)),
-            dma((2, max(count_c - 1, 1))),
-            dma((2, max(count_c - 1, 1))),
-            dma((2, max(count_c - 1, 1))),
+            dma((2, steps_c)),
+            dma((2, steps_c)),
+            dma((2, steps_c)),
         ],
         compiler_params=pltpu.CompilerParams(
-            collective_id=0, has_side_effects=True, vmem_limit_bytes=48 * 1024 * 1024
+            collective_id=0, has_side_effects=True, vmem_limit_bytes=60 * 1024 * 1024
         ),
         name="front",
     )(
         level_one, level_two, level_three, level_four, bin_weight, neck_feature, neck_pooled,
-        biases, biases[: len(bin_sides)].reshape(-1, share),
-        jnp.asarray(member, bf16), jnp.asarray(scale), jnp.asarray(spread),
+        biases, jnp.asarray(member, bf16), jnp.asarray(scale), jnp.asarray(spread),
         jnp.asarray(pick_top, bf16), jnp.asarray(pick_three, bf16),
     )
     n1, n2, n3 = w1 + 16, w2 + 16, round_up(pack3, 16)
     return pl.pallas_call(
         functools.partial(back, sizes),
         out_shape=jax.ShapeDtypeStruct((h1, w1, channels), bf16),
-        in_specs=[vmem] * 10,
+        in_specs=[hbm] * 10,
         out_specs=vmem,
-        scratch_shapes=[
+        scratch_shapes=[pltpu.VMEM(frame.shape, bf16) for frame in frames] + [
+            pltpu.VMEM(lateral_one.shape, bf16),
+            pltpu.VMEM(lateral_two.shape, bf16),
+            pltpu.VMEM(lateral_three.shape, bf16),
+            pltpu.VMEM(smooth_weight.shape, bf16),
+            pltpu.VMEM(join_weight.shape, bf16),
+            pltpu.VMEM(biases.shape, f32),
             pltpu.VMEM((h3 + 4, n3, channels), bf16),
             pltpu.VMEM((h2 + 4, n2, channels), bf16),
             pltpu.VMEM((h1 + 4, n1, channels), bf16),
@@ -517,8 +577,9 @@
             pltpu.VMEM((h2 + 2, n2, channels), bf16),
             pltpu.VMEM((h1 + 2, n1, 4 * channels), bf16),
             pltpu.VMEM((h2 + 4, n1, channels), f32),
+            dma((10,)),
         ],
-        compiler_params=pltpu.CompilerParams(vmem_limit_bytes=56 * 1024 * 1024),
+        compiler_params=pltpu.CompilerParams(vmem_limit_bytes=60 * 1024 * 1024),
         name="back",
     )(*frames, lateral_one, lateral_two, lateral_three, smooth_weight, join_weight, biases)
 

time: 66.6 us -> 37.6 us (0.56)
  local copies, waits for them, and re-layouts: 14.4 us -> 0 us
  Pallas kernels: 51.6 us -> 37.5 us
    unnamed x30 -> x0, local copies, waits for them, and re-layouts: 13.7 us -> none
    pallas_call x1, Pallas kernels: 34 us -> 22.6 us  [local(): pl.pallas_call(functools.partial(front, sizes), out_shape=(jax.ShapeDtype...]
    pallas_call x1, Pallas kernels: 17.6 us -> 14.9 us  [local(): pl.pallas_call(functools.partial(back, sizes), out_shape=jax.ShapeDtypeSt...]
    slice x1 -> x0, local copies, waits for them, and re-layouts: 0.7 us -> none  [local(): biases[:len(bin_sides)].reshape(-1, share)]
where the time goes in v2:
time: 37.6 us; the launch traced here: 37.5 us
  Pallas kernels  37.5 us (100%)
    pallas_call x1, Pallas kernels, local(): pl.pallas_call(functools.partial(front, sizes), out_shape=(jax.ShapeDtype...  22.6 us
    pallas_call x1, Pallas kernels, local(): pl.pallas_call(functools.partial(back, sizes), out_shape=jax.ShapeDtypeSt...  14.9 us

profile of v2, /device:TPU:0, one launch (start us, length us, event | category | flops | bytes accessed | tf_op | source)
XLA Modules:
  0.0 37.5 jit_solution(933421007982106770)
XLA Ops:
  0.0 22.6 %front.1 = (bf16[20,96,192]{2,1,0:T(8,128)(2,1)}, bf16[12,64,384]{2,1,0:T(8,128)(2,1)}, bf16[4,192,192]{2,1,0:T(8,128)(2,1)}, bf16[96,256]{1,0:T(8,128)(2,1)}) custom-call(bf16[16,64,192]{2,1,0:T(8,128)(2,1)} %one_h.1, bf16[8,32,384]{2,1,0:T(8,128)(2,1)} %two_h.1, bf16[4,64,192]{2,1,0:T(8,128)(2,1)} %three_h.1, bf16[2,32,384]{2,1,0:T(8,128)(2,1)} %four_h.1, ...), custom_call_target="tpu_custom_call" | custom-call | tf_op jit(solution)/shard_map/front/pallas_call | solution.py:511
  22.6 14.9 %back.1 = bf16[16,64,256]{2,1,0:T(8,128)(2,1)} custom-call(bf16[20,96,192]{2,1,0:T(8,128)(2,1)} %get-tuple-element.9.f1_h, bf16[12,64,384]{2,1,0:T(8,128)(2,1)} %get-tuple-element.10.f2_h, bf16[4,192,192]{2,1,0:T(8,128)(2,1)} %get-tuple-element.11.t3_h, bf16[96,256]{1,0:T(8,128)(2,1)} %get-tuple-element.12.top_h, bf16[192,256]{1,0:T(8,128)(2,1)} %lat1_h.1, ...), custom_call_target="tpu_custom_call" | custom-call | tf_op jit(solution)/shard_map/back/pallas_call | solution.py:561

commit v3 on v2

--- a/solution.py
+++ b/solution.py
@@ -77,6 +77,7 @@
     three, bins, neck, necked, offsets, member, scale, table, pick_top, pick_three,
     grid, send3, bin_out, bin_in, sendt, gott, ppm, out1, in1, out2, in2,
     sem_local, sem_four, sem_row, sem_col, sem_three, sem_bin, sem_top,
+    early, later,
 ):
     count_r, count_c = sizes
     row, col = lax.axis_index("row"), lax.axis_index("col")
@@ -112,6 +113,8 @@
         fetch(spread_h.at[branch, pl.ds(row * h4 * w4, (tall + 2) * w4)], table, 9),
         fetch(offsets_h, offsets, 10), fetch(necked_h, necked, 11), fetch(pick_top_h, pick_top, 12),
     ]
+
+    early()
 
     for frame, h in ((f1, h1), (f2, h2)):
         rim = jnp.zeros((2, frame.shape[1], frame.shape[2]), frame.dtype)
@@ -209,6 +212,28 @@
         bin_copies.append(copy)
     bin_in[pl.ds(col, 1)] = bin_out[pl.ds(col, 1)]
 
+    for copy in get_one:
+        copy.wait()
+    when_each(has_down, up_copies, "wait_recv")
+    when_each(has_up, down_copies, "wait_recv")
+    left_copies, right_copies = [], []
+    for number, (frame, h, w, outgoing, incoming) in enumerate(
+        ((f1, h1 + 4, w1, out1, in1), (f2, h2 + 4, w2, out2, in2))
+    ):
+        count, depth = outgoing.shape[1:]
+        block = frame[:, EDGE : 2 * EDGE].reshape(h * EDGE, depth)
+        outgoing[0] = dot(column_pick(h, count, 0, False), block).astype(jnp.bfloat16)
+        block = frame[:, w : EDGE + w].reshape(h * EDGE, depth)
+        outgoing[1] = dot(column_pick(h, count, EDGE - 2, False), block).astype(jnp.bfloat16)
+        left_copies.append(
+            remote(outgoing.at[0], incoming.at[1], sem_col, number, {"col": col - 1})
+        )
+        right_copies.append(
+            remote(outgoing.at[1], incoming.at[0], sem_col, 2 + number, {"col": col + 1})
+        )
+    when_each(has_left, left_copies, "start")
+    when_each(has_right, right_copies, "start")
+
     for copy in get_neck:
         copy.wait()
     terms = [None] * 3
@@ -217,6 +242,14 @@
         for dx in range(3):
             term = dot(window, neck[dy, dx])
             terms[dx] = term if dy == 0 else terms[dx] + term
+
+    for copy in three_copies:
+        copy.wait_recv()
+    up3 = remote(t3.at[:, halo3 : 2 * halo3], t3.at[:, halo3 + own3 :], sem_row, 4,
+                 {"row": row - 1})
+    down3 = remote(t3.at[:, own3 : own3 + halo3], t3.at[:, 0:halo3], sem_row, 5, {"row": row + 1})
+    when_each(has_up, [up3], "start")
+    when_each(has_down, [down3], "start")
 
     for copy in get_rest:
         copy.wait()
@@ -261,42 +294,6 @@
         top_copies.append(copy)
     gott[pl.ds(col, 1)] = sendt[pl.ds(col, 1)]
 
-    for copy in three_copies:
-        copy.wait_recv()
-    up3 = remote(t3.at[:, halo3 : 2 * halo3], t3.at[:, halo3 + own3 :], sem_row, 4,
-                 {"row": row - 1})
-    down3 = remote(t3.at[:, own3 : own3 + halo3], t3.at[:, 0:halo3], sem_row, 5, {"row": row + 1})
-    when_each(has_up, [up3], "start")
-    when_each(has_down, [down3], "start")
-    for copy in get_one:
-        copy.wait()
-    when_each(has_down, up_copies, "wait_recv")
-    when_each(has_up, down_copies, "wait_recv")
-    left_copies, right_copies = [], []
-    for number, (frame, h, w, outgoing, incoming) in enumerate(
-        ((f1, h1 + 4, w1, out1, in1), (f2, h2 + 4, w2, out2, in2))
-    ):
-        count, depth = outgoing.shape[1:]
-        block = frame[:, EDGE : 2 * EDGE].reshape(h * EDGE, depth)
-        outgoing[0] = dot(column_pick(h, count, 0, False), block).astype(jnp.bfloat16)
-        block = frame[:, w : EDGE + w].reshape(h * EDGE, depth)
-        outgoing[1] = dot(column_pick(h, count, EDGE - 2, False), block).astype(jnp.bfloat16)
-        left_copies.append(
-            remote(outgoing.at[0], incoming.at[1], sem_col, number, {"col": col - 1})
-        )
-        right_copies.append(
-            remote(outgoing.at[1], incoming.at[0], sem_col, 2 + number, {"col": col + 1})
-        )
-    when_each(has_left, left_copies, "start")
-    when_each(has_right, right_copies, "start")
-
-    for copy in top_copies:
-        copy.wait_recv()
-    total = gott[0].astype(jnp.float32)
-    for part in range(1, count_c):
-        total = total + gott[part].astype(jnp.float32)
-    top[...] = jnp.maximum(total + offsets[4:5], 0.0).astype(jnp.bfloat16)
-
     when_each(has_right, left_copies, "wait_recv")
     when_each(has_left, right_copies, "wait_recv")
     for frame, h, w, incoming in ((f1, h1 + 4, w1, in1), (f2, h2 + 4, w2, in2)):
@@ -307,6 +304,14 @@
         frame[:, EDGE + w :] = value.astype(jnp.bfloat16).reshape(h, EDGE, depth)
     when_each(has_down, [up3], "wait_recv")
     when_each(has_up, [down3], "wait_recv")
+    later()
+
+    for copy in top_copies:
+        copy.wait_recv()
+    total = gott[0].astype(jnp.float32)
+    for part in range(1, count_c):
+        total = total + gott[part].astype(jnp.float32)
+    top[...] = jnp.maximum(total + offsets[4:5], 0.0).astype(jnp.bfloat16)
 
     for copy in four_copies + bin_copies + three_copies + top_copies:
         copy.wait_send()
@@ -326,17 +331,9 @@
 
 
 def back(
-    sizes, f1_h, f2_h, t3_h, top_h, lat1_h, lat2_h, lat3_h, smooth_h, join_h, offsets_h, out,
-    f1, f2, t3, top, lat1, lat2, lat3, smooth, join, offsets, p3, p2, p1, s3, s2, joint, wide, sems,
+    sizes, f1, f2, t3, top, offsets, fetches, out, lat1, lat2, lat3, smooth, join,
+    p3, p2, p1, s3, s2, joint, wide, term3, term2, term1,
 ):
-    fetches = []
-    for source, target in (
-        (t3_h, t3), (lat3_h, lat3), (offsets_h, offsets), (top_h, top), (f2_h, f2), (lat2_h, lat2),
-        (f1_h, f1), (lat1_h, lat1), (smooth_h, smooth), (join_h, join),
-    ):
-        copy = pltpu.make_async_copy(source, target, sems.at[len(fetches)])
-        copy.start()
-        fetches.append(copy)
     count_r, count_c = sizes
     row, col = lax.axis_index("row"), lax.axis_index("col")
     at_top, at_bottom = row == 0, row == count_r - 1
@@ -396,17 +393,7 @@
             sums.append(total)
         return sums[1] + pltpu.roll(sums[0], 1, 0) + pltpu.roll(sums[2], size - 1, 0)
 
-    for copy in fetches[0:4]:
-        copy.wait()
-    term = None
-    share = t3.shape[2]
-    for part in range(count_c):
-        piece = dot(t3[part], lat3[part * share : (part + 1) * share])
-        term = piece if term is None else term + piece
-    term = jnp.maximum(term + offsets[7:8], 0.0).reshape(h3 + 4, pack3, channels)
-    term = jnp.concatenate(
-        [term, jnp.zeros((h3 + 4, n3 - pack3, channels), jnp.float32)], axis=1
-    )
+    term = term3
     keep = inside(-4, n3, w3)
     widen(lambda r: top[r * n4 : (r + 1) * n4],
           column_matrix(col, w3, -4, n3, w4, -4, n4, 2, w3 * count_c), h4, 2)
@@ -414,26 +401,20 @@
         value = jnp.where(keep[0], term[t + 2] + interpolate(t, 2, 2, n3), 0.0)
         store_row(p3, t + 2, value, t, h3)
 
-    for copy in fetches[4:6]:
-        copy.wait()
-    term = dot(f2[...].reshape((h2 + 4) * f2.shape[1], f2.shape[2]), lat2[...])
-    term = jnp.maximum(term + offsets[6:7], 0.0).reshape(h2 + 4, f2.shape[1], channels)
+    term = term2
     keep = inside(-8, n2, w2)
     widen(lambda r: p3[r], column_matrix(col, w2, -8, n2, w3, -4, n3, 2, w2 * count_c), h3, 2)
     for t in range(-2, h2 + 2):
-        value = jnp.where(keep[0], term[t + 2, 8 : 8 + n2] + interpolate(t, 2, 2, n2), 0.0)
+        value = jnp.where(keep[0], term[t + 2] + interpolate(t, 2, 2, n2), 0.0)
         store_row(p2, t + 2, value, t, h2)
 
-    for copy in fetches[6:8]:
-        copy.wait()
     keep = inside(-8, n1, w1)
     widen(lambda r: p2[r], column_matrix(col, w1, -8, n1, w2, -8, n2, 2, w1 * count_c), h2, 2)
     for t in range(-2, h1 + 2):
-        term = jnp.maximum(dot(f1[t + 2], lat1[...]) + offsets[5:6], 0.0)
-        value = jnp.where(keep[0], term[8 : 8 + n1] + interpolate(t, 2, 2, n1), 0.0)
+        value = jnp.where(keep[0], term1[t + 2] + interpolate(t, 2, 2, n1), 0.0)
         store_row(p1, t + 2, value, t, h1)
 
-    fetches[8].wait()
+    fetches[3].wait()
     value = taps(lambda dy: p3[dy : dy + h3 + 2].reshape((h3 + 2) * n3, channels),
                  lambda dy, dx: smooth[2, dy, dx], n3, h3 + 2)
     s3[...] = jnp.maximum(value + offsets[10:11], 0.0).astype(jnp.bfloat16).reshape(s3.shape)
@@ -472,7 +453,7 @@
         for t in range(-1, h1 + 1):
             store_row(joint, t + 1, interpolate(t, factor, border, n1), t, h1, lanes)
 
-    fetches[9].wait()
+    fetches[4].wait()
     rows = 4
     @pl.loop(0, h1 // rows)
     def _(block):
@@ -482,6 +463,50 @@
         )
         value = jnp.maximum(value + offsets[11:12], 0.0).reshape(rows, n1, channels)
         out[pl.ds(block * rows, rows)] = value[:, 8 : 8 + w1].astype(jnp.bfloat16)
+
+
+def laterals(f1, f2, t3, offsets, fetches, lat1, lat2, lat3, term3, term2, term1):
+    for copy in fetches[0:3]:
+        copy.wait()
+    share = t3.shape[2]
+    term = None
+    for part in range(t3.shape[0]):
+        piece = dot(t3[part], lat3[part * share : (part + 1) * share])
+        term = piece if term is None else term + piece
+    rows, width, channels = term3.shape
+    packed = t3.shape[1] // rows
+    term3[:, 0:packed] = jnp.maximum(term + offsets[7:8], 0.0).reshape(rows, packed, channels)
+    term3[:, packed:] = jnp.zeros((rows, width - packed, channels), jnp.float32)
+    for frame, weight, line, target in ((f2, lat2, 6, term2), (f1, lat1, 5, term1)):
+        for r in range(frame.shape[0]):
+            term = jnp.maximum(dot(frame[r], weight[...]) + offsets[line : line + 1], 0.0)
+            target[r] = term[8 : 8 + target.shape[1]]
+
+
+def head(sizes, *refs):
+    inputs, (lat1_h, lat2_h, lat3_h, smooth_h, join_h), out = refs[:13], refs[13:18], refs[18]
+    f1, f2, t3, top = refs[19:23]
+    scratch, weights, maps, terms, sems = (
+        refs[23:51], refs[51:56], refs[56:63], refs[63:66], refs[66]
+    )
+    lat1, lat2, lat3, smooth, join = weights
+    offsets = scratch[4]
+    fetches = [
+        pltpu.make_async_copy(source, target, sems.at[number])
+        for number, (source, target) in enumerate((
+            (lat3_h, lat3), (lat2_h, lat2), (lat1_h, lat1), (smooth_h, smooth), (join_h, join),
+        ))
+    ]
+
+    def early():
+        for copy in fetches:
+            copy.start()
+
+    def later():
+        laterals(f1, f2, t3, offsets, fetches, lat1, lat2, lat3, *terms)
+
+    front(sizes, *inputs, f1, f2, t3, top, *scratch, early, later)
+    back(sizes, f1, f2, t3, top, offsets, fetches, out, *weights, *maps, *terms)
 
 
 def local(
@@ -508,17 +533,17 @@
     dma = pltpu.SemaphoreType.DMA
     steps_r, steps_c = max(count_r - 1, 1), max(count_c - 1, 1)
     column1, column2 = round_up(2 * (h1 + 4), 16), round_up(2 * (h2 + 4), 16)
-    frames = pl.pallas_call(
-        functools.partial(front, sizes),
-        out_shape=(
-            jax.ShapeDtypeStruct((h1 + 4, w1 + 2 * EDGE, c1), bf16),
-            jax.ShapeDtypeStruct((h2 + 4, w2 + 2 * EDGE, c2), bf16),
-            jax.ShapeDtypeStruct((count_c, (h3 + 4) * pack3, c3), bf16),
-            jax.ShapeDtypeStruct(((h4 + 4) * pack4, channels), bf16),
-        ),
-        in_specs=[hbm] * 13,
-        out_specs=[vmem] * 4,
+    n1, n2, n3 = w1 + 16, w2 + 16, round_up(pack3, 16)
+    return pl.pallas_call(
+        functools.partial(head, sizes),
+        out_shape=jax.ShapeDtypeStruct((h1, w1, channels), bf16),
+        in_specs=[hbm] * 18,
+        out_specs=vmem,
         scratch_shapes=[
+            pltpu.VMEM((h1 + 4, w1 + 2 * EDGE, c1), bf16),
+            pltpu.VMEM((h2 + 4, w2 + 2 * EDGE, c2), bf16),
+            pltpu.VMEM((count_c, (h3 + 4) * pack3, c3), bf16),
+            pltpu.VMEM(((h4 + 4) * pack4, channels), bf16),
             pltpu.VMEM(level_three.shape, bf16),
             pltpu.VMEM(bin_weight.shape, bf16),
             pltpu.VMEM(neck_feature.shape, bf16),
@@ -547,29 +572,11 @@
             dma((2, steps_c)),
             dma((2, steps_c)),
             dma((2, steps_c)),
-        ],
-        compiler_params=pltpu.CompilerParams(
-            collective_id=0, has_side_effects=True, vmem_limit_bytes=60 * 1024 * 1024
-        ),
-        name="front",
-    )(
-        level_one, level_two, level_three, level_four, bin_weight, neck_feature, neck_pooled,
-        biases, jnp.asarray(member, bf16), jnp.asarray(scale), jnp.asarray(spread),
-        jnp.asarray(pick_top, bf16), jnp.asarray(pick_three, bf16),
-    )
-    n1, n2, n3 = w1 + 16, w2 + 16, round_up(pack3, 16)
-    return pl.pallas_call(
-        functools.partial(back, sizes),
-        out_shape=jax.ShapeDtypeStruct((h1, w1, channels), bf16),
-        in_specs=[hbm] * 10,
-        out_specs=vmem,
-        scratch_shapes=[pltpu.VMEM(frame.shape, bf16) for frame in frames] + [
             pltpu.VMEM(lateral_one.shape, bf16),
             pltpu.VMEM(lateral_two.shape, bf16),
             pltpu.VMEM(lateral_three.shape, bf16),
             pltpu.VMEM(smooth_weight.shape, bf16),
             pltpu.VMEM(join_weight.shape, bf16),
-            pltpu.VMEM(biases.shape, f32),
             pltpu.VMEM((h3 + 4, n3, channels), bf16),
             pltpu.VMEM((h2 + 4, n2, channels), bf16),
             pltpu.VMEM((h1 + 4, n1, channels), bf16),
@@ -577,11 +584,21 @@
             pltpu.VMEM((h2 + 2, n2, channels), bf16),
             pltpu.VMEM((h1 + 2, n1, 4 * channels), bf16),
             pltpu.VMEM((h2 + 4, n1, channels), f32),
-            dma((10,)),
+            pltpu.VMEM((h3 + 4, n3, channels), f32),
+            pltpu.VMEM((h2 + 4, n2, channels), f32),
+            pltpu.VMEM((h1 + 4, n1, channels), f32),
+            dma((5,)),
         ],
-        compiler_params=pltpu.CompilerParams(vmem_limit_bytes=60 * 1024 * 1024),
-        name="back",
-    )(*frames, lateral_one, lateral_two, lateral_three, smooth_weight, join_weight, biases)
+        compiler_params=pltpu.CompilerParams(
+            collective_id=0, has_side_effects=True, vmem_limit_bytes=60 * 1024 * 1024
+        ),
+        name="head",
+    )(
+        level_one, level_two, level_three, level_four, bin_weight, neck_feature, neck_pooled,
+        biases, jnp.asarray(member, bf16), jnp.asarray(scale), jnp.asarray(spread),
+        jnp.asarray(pick_top, bf16), jnp.asarray(pick_three, bf16),
+        lateral_one, lateral_two, lateral_three, smooth_weight, join_weight,
+    )
 
 
 def solution(mesh):

time: 37.6 us -> 35.5 us (0.944)
  Pallas kernels: 37.5 us -> 33.5 us
  local copies, waits for them, and re-layouts: 0 us -> 1.88 us
    pallas_call x2 -> x1, Pallas kernels: 37.5 us -> 33.5 us  [local(): pl.pallas_call(functools.partial(head, sizes), out_shape=jax.ShapeDtypeSt...]
    unnamed x0 -> x1, local copies, waits for them, and re-layouts: none -> 1.88 us
where the time goes in v3:
time: 35.5 us; the launch traced here: 35.4 us
  Pallas kernels  33.5 us (94%)
  local copies, waits for them, and re-layouts  1.88 us (5%)
    pallas_call x1, Pallas kernels, local(): pl.pallas_call(functools.partial(head, sizes), out_shape=jax.ShapeDtypeSt...  33.5 us
    unnamed x1, local copies, waits for them, and re-layouts  1.88 us

profile of v3, /device:TPU:0, one launch (start us, length us, event | category | flops | bytes accessed | tf_op | source)
XLA Modules:
  0.0 35.4 jit_solution(6543944061538387809)
XLA Ops:
  0.0 33.5 %head.1 = bf16[16,64,256]{2,1,0:T(8,128)(2,1)} custom-call(bf16[16,64,192]{2,1,0:T(8,128)(2,1)} %refs_0_.1, bf16[8,32,384]{2,1,0:T(8,128)(2,1)} %refs_1_.1, bf16[4,64,192]{2,1,0:T(8,128)(2,1)} %refs_2_.1, bf16[2,32,384]{2,1,0:T(8,128)(2,1)} %refs_3_.1, bf16[4,384,256]{2,1,0:T(8,128)(2,1)} %refs_4_.1, bf16[3,3,384,256]{3,2,1,0:T(8,128)(2,1)} %refs_5_.1, ...), custom_call_target="tpu_custom_call" | custom-call | tf_op jit(solution)/shard_map/head/pallas_call | solution.py:537
  33.5 1.9 %copy.20 = bf16[16,64,256]{2,1,0:T(8,128)(2,1)} copy(bf16[16,64,256]{2,1,0:T(8,128)(2,1)} %head.1) | data formatting | bytes 1048576
